TPU v7x, 256 devices: a whole 4x4x8 slice. The times are simulated.
256 devices in a mesh: seq: 32 (over z, x), head: 8 (over y, core).
Axes of the slice: x: 4, y: 4, z: 8, core: 2. Of those that a mesh axis runs over, the one named last changes fastest.
Arguments:
- query: bfloat16 [16384, 16, 128], P('seq', 'head'), may hold values from -60 to 60
- key: bfloat16 [16384, 16, 128], P('seq', 'head'), may hold values from -6 to 6
- value: bfloat16 [16384, 16, 128], P('seq', 'head'), may hold values from -6 to 6
- reflect: bfloat16 [16384, 16, 128], P('seq', 'head'), may hold values from -8 to 8
- block_mask: int32 [16, 128, 128], P('head'), may hold values from 0 to 1, as said below
- out_weight: bfloat16 [2048, 2048], P('head'), may hold values from -0.125 to 0.125
Outputs:
- mixed: bfloat16 [16384, 2048], P('seq', 'head')
Inputs may be any that keep to these rules, and one draw needn't show every extreme that they name: block_mask[h, b, b] = 1 for every head h and block b.
All inputs are finite; a program needn't handle non-finite values.
Results may differ from a plain program's by a relative error of at most 0.011.
The roundings to bfloat16 on the way count: a program that leaves them out, or rounds other values in their place, can miss the bound.
Values may be sent and summed in bfloat16 or wider, within the bound.
No kernel may reach another device: no remote copies, remote signals or barrier semaphores. Data moves between devices by JAX's collectives and lax.ppermute only.
A program may use at most 64 MiB of HBM per device.

v0:
```python
from functools import partial
import math

import jax
import jax.numpy as jnp
from jax import lax
from jax.sharding import PartitionSpec as P

BLK = 128


HIGH = lax.Precision.HIGHEST
EPSILON = 1e-06
FLOOR_SCORE = -1e30


def carried_in(value, axis, join, neutral):
    count, mine = (lax.axis_size(axis), lax.axis_index(axis))
    pieces = lax.all_gather(value, axis)
    total = jnp.full_like(value, 0) + jnp.asarray(neutral, value.dtype)

    def hop(position, total):
        longer = join(total, pieces[position])
        return jnp.where(position < mine, longer, total)

    return lax.fori_loop(0, count - 1, hop, total)


def normalize_rows(values):
    return values * lax.rsqrt(jnp.sum(values * values, axis=-1, keepdims=True) + EPSILON)


def to_blocks(values, count):
    tokens, heads, features = values.shape
    return values.astype(jnp.float32).reshape(count, BLK, heads, features).transpose(2, 0, 1, 3)


def upper_inverse(strict_upper):
    block_size = strict_upper.shape[-1]
    identity = jnp.eye(block_size, dtype=jnp.float32)
    power = -2.0 * strict_upper
    result = identity + power
    steps = block_size.bit_length() - 1
    for step in range(steps - 1):
        power = jnp.einsum("...ab,...bc->...ac", power, power, precision=HIGH)
        result = jnp.einsum("...ab,...bc->...ac", result, identity + power, precision=HIGH)
    return 2.0 * result


def block_factors(unit_dirs):
    feature_width = unit_dirs.shape[-1]
    intersections = jnp.einsum("...ad,...bd->...ab", unit_dirs, unit_dirs, precision=HIGH)
    triangle = upper_inverse(jnp.triu(intersections, 1))
    spread = jnp.einsum("...ab,...be->...ae", triangle, unit_dirs, precision=HIGH)
    block_whole = jnp.eye(feature_width, dtype=jnp.float32) - jnp.einsum(
        "...ad,...ae->...de", unit_dirs, spread, precision=HIGH
    )
    return (triangle, block_whole)


def apply_local(row_data, unit_dirs, triangle):
    block_size = row_data.shape[-2]
    projected = jnp.einsum("...md,...kd->...mk", row_data, unit_dirs, precision=HIGH)
    lower_mask = jnp.tril(jnp.ones((block_size, block_size), jnp.float32))
    coefficients = jnp.einsum(
        "...mk,...rk->...mr", projected * lower_mask, triangle, precision=HIGH
    )
    return row_data - jnp.einsum("...mr,...rd->...md", coefficients, unit_dirs, precision=HIGH)


def chain_product(earlier, later):
    return jnp.einsum("hij,hjk->hik", earlier, later, precision=HIGH)


def keep_state(carried):
    return carried


def attend_update(carried, queries, query_start, keys_part, values_part, key_start, mask_local):
    best_old, total_old, accum_old = carried
    heads, count_q, features = queries.shape
    count_k = keys_part.shape[0]
    scores = jnp.einsum(
        "hqd,khd->hqk", queries, keys_part, preferred_element_type=jnp.float32
    ) * features ** (-0.5)
    query_pos = query_start + lax.iota(jnp.int32, count_q)
    key_pos = key_start + lax.iota(jnp.int32, count_k)
    block_part = lax.dynamic_slice(
        mask_local,
        (jnp.int32(0), query_start // BLK, key_start // BLK),
        (heads, count_q // BLK, count_k // BLK),
    )
    block_full = jnp.broadcast_to(
        block_part[:, :, None, :, None] == 1, (heads, count_q // BLK, BLK, count_k // BLK, BLK)
    ).reshape(heads, count_q, count_k)
    allowed = block_full & (key_pos[None, None, :] <= query_pos[None, :, None])
    best_new = jnp.maximum(best_old, jnp.max(jnp.where(allowed, scores, FLOOR_SCORE), axis=-1))
    factor = jnp.exp(best_old - best_new)
    weights = jnp.where(allowed, jnp.exp(scores - best_new[..., None]), 0.0)
    total_new = total_old * factor + jnp.sum(weights, axis=-1)
    accum_new = accum_old * factor[..., None] + jnp.einsum(
        "hqk,khd->hqd",
        weights.astype(jnp.bfloat16),
        values_part,
        preferred_element_type=jnp.float32,
    )
    return (best_new, total_new, accum_new)


def fresh_state(queries):
    shape = queries.shape[:2]
    return (
        jnp.full(shape, FLOOR_SCORE, jnp.float32),
        jnp.zeros(shape, jnp.float32),
        jnp.zeros(queries.shape, jnp.float32),
    )


def on_device(query, key, value, reflect, block_mask, out_weight):
    tokens, heads, features = query.shape
    count = tokens // BLK
    here = lax.axis_index("seq")
    unit_dirs = normalize_rows(to_blocks(reflect, count))
    triangle, block_whole = block_factors(unit_dirs)
    local_query = apply_local(to_blocks(query, count), unit_dirs, triangle)
    local_key = apply_local(to_blocks(key, count), unit_dirs, triangle)
    identity = jnp.broadcast_to(jnp.eye(features, dtype=jnp.float32), (heads, features, features))

    def advance(frame, blockmat):
        return (chain_product(frame, blockmat), frame)

    shard_total, frames_before = lax.scan(advance, identity, block_whole.transpose(1, 0, 2, 3))
    prefix = carried_in(shard_total, "seq", chain_product, identity)
    frames = jnp.einsum("hij,bhjk->hbik", prefix, frames_before, precision=HIGH)
    rotated_query = (
        jnp.einsum("hbmd,hbed->hbme", local_query, frames, precision=HIGH)
        .reshape(heads, tokens, features)
        .astype(jnp.bfloat16)
    )
    rotated_key = (
        jnp.einsum("hbmd,hbed->hbme", local_key, frames, precision=HIGH)
        .astype(jnp.bfloat16)
        .transpose(1, 2, 0, 3)
        .reshape(tokens, heads, features)
    )
    groups = ((rotated_query, here * tokens),)
    starts = tuple((fresh_state(group[0]) for group in groups))
    keys_all = lax.all_gather(rotated_key, "seq", axis=0, tiled=True)
    values_all = lax.all_gather(value, "seq", axis=0, tiled=True)
    span = math.gcd(keys_all.shape[0], tokens)

    def visit(position, current):
        offset = position * span
        keys_part = lax.dynamic_slice_in_dim(keys_all, offset, span, 0)
        values_part = lax.dynamic_slice_in_dim(values_all, offset, span, 0)
        updated = []
        for group, carried in zip(groups, current):
            queries, query_start = group
            last_query = query_start + queries.shape[1] - 1
            update_fn = partial(
                attend_update,
                queries=queries,
                query_start=query_start,
                keys_part=keys_part,
                values_part=values_part,
                key_start=offset,
                mask_local=block_mask,
            )
            updated.append(lax.cond(offset <= last_query, update_fn, keep_state, carried))
        return tuple(updated)

    finals = lax.fori_loop(0, keys_all.shape[0] // span, visit, starts)
    attended = [
        (accum / total_sum[..., None]).astype(jnp.bfloat16)
        for best_value, total_sum, accum in finals
    ]
    combined = attended[0]
    weight_heads = out_weight.reshape(heads, features, out_weight.shape[1])
    head_terms = jnp.einsum(
        "hld,hde->le", combined, weight_heads, preferred_element_type=jnp.float32
    )
    return lax.psum_scatter(head_terms, "head", scatter_dimension=1, tiled=True).astype(
        jnp.bfloat16
    )


def solution(mesh):
    in_specs = (
        P("seq", "head", None),
        P("seq", "head", None),
        P("seq", "head", None),
        P("seq", "head", None),
        P("head", None, None),
        P("head", None),
    )
    out_specs = P("seq", "head")
    return jax.shard_map(
        on_device, mesh=mesh, in_specs=in_specs, out_specs=out_specs, check_vma=False
    )
```

profile of v0, /device:TPU:224, one launch (start us, length us, event | category | flops | bytes accessed | tf_op | source)
XLA Modules:
  0.0 574.2 jit_solution(836294105609138359)
XLA Ops:
  28.0 77.6 %all-gather.9.cloned.1.call-done = f32[64,128,128]{2,1,0:T(8,128)} async-done(((f32[2,128,128]{2,1,0:T(8,128)}), f32[64,128,128]{2,1,0:T(8,128)}) %all-gather.9.cloned.1.call-update) | async-done | bytes 4194320 | tf_op jit(solution)/shard_map/all_gather | solution.py:19
  105.6 41.8 %while.45 = (s32[]{:T(128)}, f32[2,128,128]{1,2,0:T(8,128)S(1)}, s32[]{:T(128)}, f32[32,2,128,128]{3,2,1,0:T(8,128)}, s32[]{:T(128)}) while((s32[]{:T(128)}, f32[2,128,128]{1,2,0:T(8,128)S(1)}, s32[]{:T(128)}, f32[32,2,128,128]{3,2,1,0:T(8,128)}, s32[]{:T(128)}) %tuple.122), condition=%wide.region_4.5_spmd, body=%wide.region_3.4_spmd.sunk | while | flops 50364416 | bytes 786515 | solution.py:26
  156.5 46.3 %all-gather.7.cloned.1.call-done = bf16[16384,2,128]{2,0,1:T(8,128)(2,1)} async-done(((bf16[512,2,128]{2,0,1:T(8,128)(2,1)}), bf16[16384,2,128]{2,0,1:T(8,128)(2,1)}) %all-gather.7.cloned.1.call-update) | async-done | bytes 8388624 | tf_op jit(solution)/shard_map/all_gather | solution.py:149
  202.8 98.0 %all-gather.5.cloned.1.call-done = bf16[16384,2,128]{2,0,1:T(8,128)(2,1)} async-done(((bf16[512,2,128]{2,0,1:T(8,128)(2,1)}), bf16[16384,2,128]{2,0,1:T(8,128)(2,1)}) %all-gather.5.cloned.1.call-update) | async-done | bytes 8388624 | tf_op jit(solution)/shard_map/all_gather | solution.py:148
  300.8 204.0 %while.46 = (s32[]{:T(128)}, f32[2,512]{1,0:T(2,128)S(1)}, f32[2,512]{1,0:T(2,128)S(1)}, f32[2,512,128]{2,1,0:T(8,128)S(1)}, s32[]{:T(128)}, /*index=5*/s32[]{:T...) while((s32[]{:T(128)}, f32[2,512]{1,0:T(2,128)S(1)}, ...), condition=%wide.region_10.11_spmd, body=%wide.region_5.10_spmd.sunk | while | flops 276302912 | bytes 12395376 | solution.py:172
  300.9 7.0 %conditional.2 = ((f32[2,512]{1,0:T(2,128)S(1)}, f32[2,512]{1,0:T(2,128)S(1)}, f32[2,512,128]{2,1,0:T(8,128)S(1)})) conditional(s32[]{:T(128)} %convert_element_type.79, (f32[2,512]{1,0:T(2,128)S(1)}, f32[2,512]{1,0:T(2,128)S(1)}, f32[2,512,128]{2,1,0:T(8,128)S(1)}) %tuple.98, (s32[]{:T(128)}, s32[]{:T(128)}, s32[2,128,128]{1,2,0:T(8,128)}, ...), branch_computations={%region_6.6_spmd, %region_7.9_spmd} | conditional | flops 276302912 | bytes 12395137 | solution.py:169
  307.9 7.0 %conditional.2 = ((f32[2,512]{1,0:T(2,128)S(1)}, f32[2,512]{1,0:T(2,128)S(1)}, f32[2,512,128]{2,1,0:T(8,128)S(1)})) conditional(s32[]{:T(128)} %convert_element_type.79, (f32[2,512]{1,0:T(2,128)S(1)}, f32[2,512]{1,0:T(2,128)S(1)}, f32[2,512,128]{2,1,0:T(8,128)S(1)}) %tuple.98, (s32[]{:T(128)}, s32[]{:T(128)}, s32[2,128,128]{1,2,0:T(8,128)}, ...), branch_computations={%region_6.6_spmd, %region_7.9_spmd} | conditional | flops 276302912 | bytes 12395137 | solution.py:169
  314.9 7.0 %conditional.2 = ((f32[2,512]{1,0:T(2,128)S(1)}, f32[2,512]{1,0:T(2,128)S(1)}, f32[2,512,128]{2,1,0:T(8,128)S(1)})) conditional(s32[]{:T(128)} %convert_element_type.79, (f32[2,512]{1,0:T(2,128)S(1)}, f32[2,512]{1,0:T(2,128)S(1)}, f32[2,512,128]{2,1,0:T(8,128)S(1)}) %tuple.98, (s32[]{:T(128)}, s32[]{:T(128)}, s32[2,128,128]{1,2,0:T(8,128)}, ...), branch_computations={%region_6.6_spmd, %region_7.9_spmd} | conditional | flops 276302912 | bytes 12395137 | solution.py:169
  322.0 7.0 %conditional.2 = ((f32[2,512]{1,0:T(2,128)S(1)}, f32[2,512]{1,0:T(2,128)S(1)}, f32[2,512,128]{2,1,0:T(8,128)S(1)})) conditional(s32[]{:T(128)} %convert_element_type.79, (f32[2,512]{1,0:T(2,128)S(1)}, f32[2,512]{1,0:T(2,128)S(1)}, f32[2,512,128]{2,1,0:T(8,128)S(1)}) %tuple.98, (s32[]{:T(128)}, s32[]{:T(128)}, s32[2,128,128]{1,2,0:T(8,128)}, ...), branch_computations={%region_6.6_spmd, %region_7.9_spmd} | conditional | flops 276302912 | bytes 12395137 | solution.py:169
  329.0 7.0 %conditional.2 = ((f32[2,512]{1,0:T(2,128)S(1)}, f32[2,512]{1,0:T(2,128)S(1)}, f32[2,512,128]{2,1,0:T(8,128)S(1)})) conditional(s32[]{:T(128)} %convert_element_type.79, (f32[2,512]{1,0:T(2,128)S(1)}, f32[2,512]{1,0:T(2,128)S(1)}, f32[2,512,128]{2,1,0:T(8,128)S(1)}) %tuple.98, (s32[]{:T(128)}, s32[]{:T(128)}, s32[2,128,128]{1,2,0:T(8,128)}, ...), branch_computations={%region_6.6_spmd, %region_7.9_spmd} | conditional | flops 276302912 | bytes 12395137 | solution.py:169
  336.0 7.0 %conditional.2 = ((f32[2,512]{1,0:T(2,128)S(1)}, f32[2,512]{1,0:T(2,128)S(1)}, f32[2,512,128]{2,1,0:T(8,128)S(1)})) conditional(s32[]{:T(128)} %convert_element_type.79, (f32[2,512]{1,0:T(2,128)S(1)}, f32[2,512]{1,0:T(2,128)S(1)}, f32[2,512,128]{2,1,0:T(8,128)S(1)}) %tuple.98, (s32[]{:T(128)}, s32[]{:T(128)}, s32[2,128,128]{1,2,0:T(8,128)}, ...), branch_computations={%region_6.6_spmd, %region_7.9_spmd} | conditional | flops 276302912 | bytes 12395137 | solution.py:169
  343.0 7.0 %conditional.2 = ((f32[2,512]{1,0:T(2,128)S(1)}, f32[2,512]{1,0:T(2,128)S(1)}, f32[2,512,128]{2,1,0:T(8,128)S(1)})) conditional(s32[]{:T(128)} %convert_element_type.79, (f32[2,512]{1,0:T(2,128)S(1)}, f32[2,512]{1,0:T(2,128)S(1)}, f32[2,512,128]{2,1,0:T(8,128)S(1)}) %tuple.98, (s32[]{:T(128)}, s32[]{:T(128)}, s32[2,128,128]{1,2,0:T(8,128)}, ...), branch_computations={%region_6.6_spmd, %region_7.9_spmd} | conditional | flops 276302912 | bytes 12395137 | solution.py:169
  350.1 7.0 %conditional.2 = ((f32[2,512]{1,0:T(2,128)S(1)}, f32[2,512]{1,0:T(2,128)S(1)}, f32[2,512,128]{2,1,0:T(8,128)S(1)})) conditional(s32[]{:T(128)} %convert_element_type.79, (f32[2,512]{1,0:T(2,128)S(1)}, f32[2,512]{1,0:T(2,128)S(1)}, f32[2,512,128]{2,1,0:T(8,128)S(1)}) %tuple.98, (s32[]{:T(128)}, s32[]{:T(128)}, s32[2,128,128]{1,2,0:T(8,128)}, ...), branch_computations={%region_6.6_spmd, %region_7.9_spmd} | conditional | flops 276302912 | bytes 12395137 | solution.py:169
  357.1 7.0 %conditional.2 = ((f32[2,512]{1,0:T(2,128)S(1)}, f32[2,512]{1,0:T(2,128)S(1)}, f32[2,512,128]{2,1,0:T(8,128)S(1)})) conditional(s32[]{:T(128)} %convert_element_type.79, (f32[2,512]{1,0:T(2,128)S(1)}, f32[2,512]{1,0:T(2,128)S(1)}, f32[2,512,128]{2,1,0:T(8,128)S(1)}) %tuple.98, (s32[]{:T(128)}, s32[]{:T(128)}, s32[2,128,128]{1,2,0:T(8,128)}, ...), branch_computations={%region_6.6_spmd, %region_7.9_spmd} | conditional | flops 276302912 | bytes 12395137 | solution.py:169
  364.1 7.0 %conditional.2 = ((f32[2,512]{1,0:T(2,128)S(1)}, f32[2,512]{1,0:T(2,128)S(1)}, f32[2,512,128]{2,1,0:T(8,128)S(1)})) conditional(s32[]{:T(128)} %convert_element_type.79, (f32[2,512]{1,0:T(2,128)S(1)}, f32[2,512]{1,0:T(2,128)S(1)}, f32[2,512,128]{2,1,0:T(8,128)S(1)}) %tuple.98, (s32[]{:T(128)}, s32[]{:T(128)}, s32[2,128,128]{1,2,0:T(8,128)}, ...), branch_computations={%region_6.6_spmd, %region_7.9_spmd} | conditional | flops 276302912 | bytes 12395137 | solution.py:169
  371.2 7.0 %conditional.2 = ((f32[2,512]{1,0:T(2,128)S(1)}, f32[2,512]{1,0:T(2,128)S(1)}, f32[2,512,128]{2,1,0:T(8,128)S(1)})) conditional(s32[]{:T(128)} %convert_element_type.79, (f32[2,512]{1,0:T(2,128)S(1)}, f32[2,512]{1,0:T(2,128)S(1)}, f32[2,512,128]{2,1,0:T(8,128)S(1)}) %tuple.98, (s32[]{:T(128)}, s32[]{:T(128)}, s32[2,128,128]{1,2,0:T(8,128)}, ...), branch_computations={%region_6.6_spmd, %region_7.9_spmd} | conditional | flops 276302912 | bytes 12395137 | solution.py:169
  378.2 7.0 %conditional.2 = ((f32[2,512]{1,0:T(2,128)S(1)}, f32[2,512]{1,0:T(2,128)S(1)}, f32[2,512,128]{2,1,0:T(8,128)S(1)})) conditional(s32[]{:T(128)} %convert_element_type.79, (f32[2,512]{1,0:T(2,128)S(1)}, f32[2,512]{1,0:T(2,128)S(1)}, f32[2,512,128]{2,1,0:T(8,128)S(1)}) %tuple.98, (s32[]{:T(128)}, s32[]{:T(128)}, s32[2,128,128]{1,2,0:T(8,128)}, ...), branch_computations={%region_6.6_spmd, %region_7.9_spmd} | conditional | flops 276302912 | bytes 12395137 | solution.py:169
  385.2 7.0 %conditional.2 = ((f32[2,512]{1,0:T(2,128)S(1)}, f32[2,512]{1,0:T(2,128)S(1)}, f32[2,512,128]{2,1,0:T(8,128)S(1)})) conditional(s32[]{:T(128)} %convert_element_type.79, (f32[2,512]{1,0:T(2,128)S(1)}, f32[2,512]{1,0:T(2,128)S(1)}, f32[2,512,128]{2,1,0:T(8,128)S(1)}) %tuple.98, (s32[]{:T(128)}, s32[]{:T(128)}, s32[2,128,128]{1,2,0:T(8,128)}, ...), branch_computations={%region_6.6_spmd, %region_7.9_spmd} | conditional | flops 276302912 | bytes 12395137 | solution.py:169
  392.3 7.0 %conditional.2 = ((f32[2,512]{1,0:T(2,128)S(1)}, f32[2,512]{1,0:T(2,128)S(1)}, f32[2,512,128]{2,1,0:T(8,128)S(1)})) conditional(s32[]{:T(128)} %convert_element_type.79, (f32[2,512]{1,0:T(2,128)S(1)}, f32[2,512]{1,0:T(2,128)S(1)}, f32[2,512,128]{2,1,0:T(8,128)S(1)}) %tuple.98, (s32[]{:T(128)}, s32[]{:T(128)}, s32[2,128,128]{1,2,0:T(8,128)}, ...), branch_computations={%region_6.6_spmd, %region_7.9_spmd} | conditional | flops 276302912 | bytes 12395137 | solution.py:169
  399.3 7.0 %conditional.2 = ((f32[2,512]{1,0:T(2,128)S(1)}, f32[2,512]{1,0:T(2,128)S(1)}, f32[2,512,128]{2,1,0:T(8,128)S(1)})) conditional(s32[]{:T(128)} %convert_element_type.79, (f32[2,512]{1,0:T(2,128)S(1)}, f32[2,512]{1,0:T(2,128)S(1)}, f32[2,512,128]{2,1,0:T(8,128)S(1)}) %tuple.98, (s32[]{:T(128)}, s32[]{:T(128)}, s32[2,128,128]{1,2,0:T(8,128)}, ...), branch_computations={%region_6.6_spmd, %region_7.9_spmd} | conditional | flops 276302912 | bytes 12395137 | solution.py:169
  406.3 7.0 %conditional.2 = ((f32[2,512]{1,0:T(2,128)S(1)}, f32[2,512]{1,0:T(2,128)S(1)}, f32[2,512,128]{2,1,0:T(8,128)S(1)})) conditional(s32[]{:T(128)} %convert_element_type.79, (f32[2,512]{1,0:T(2,128)S(1)}, f32[2,512]{1,0:T(2,128)S(1)}, f32[2,512,128]{2,1,0:T(8,128)S(1)}) %tuple.98, (s32[]{:T(128)}, s32[]{:T(128)}, s32[2,128,128]{1,2,0:T(8,128)}, ...), branch_computations={%region_6.6_spmd, %region_7.9_spmd} | conditional | flops 276302912 | bytes 12395137 | solution.py:169
  413.4 7.0 %conditional.2 = ((f32[2,512]{1,0:T(2,128)S(1)}, f32[2,512]{1,0:T(2,128)S(1)}, f32[2,512,128]{2,1,0:T(8,128)S(1)})) conditional(s32[]{:T(128)} %convert_element_type.79, (f32[2,512]{1,0:T(2,128)S(1)}, f32[2,512]{1,0:T(2,128)S(1)}, f32[2,512,128]{2,1,0:T(8,128)S(1)}) %tuple.98, (s32[]{:T(128)}, s32[]{:T(128)}, s32[2,128,128]{1,2,0:T(8,128)}, ...), branch_computations={%region_6.6_spmd, %region_7.9_spmd} | conditional | flops 276302912 | bytes 12395137 | solution.py:169
  420.4 7.0 %conditional.2 = ((f32[2,512]{1,0:T(2,128)S(1)}, f32[2,512]{1,0:T(2,128)S(1)}, f32[2,512,128]{2,1,0:T(8,128)S(1)})) conditional(s32[]{:T(128)} %convert_element_type.79, (f32[2,512]{1,0:T(2,128)S(1)}, f32[2,512]{1,0:T(2,128)S(1)}, f32[2,512,128]{2,1,0:T(8,128)S(1)}) %tuple.98, (s32[]{:T(128)}, s32[]{:T(128)}, s32[2,128,128]{1,2,0:T(8,128)}, ...), branch_computations={%region_6.6_spmd, %region_7.9_spmd} | conditional | flops 276302912 | bytes 12395137 | solution.py:169
  507.7 58.2 %reduce-scatter.2.cloned.1.call-done = f32[512,256]{1,0:T(8,128)} async-done(((f32[512,2048]{1,0:T(8,128)}), f32[512,256]{1,0:T(8,128)}) %reduce-scatter.2.cloned.1.call-update) | async-done | bytes 524304 | tf_op jit(solution)/shard_map/reduce_scatter | solution.py:182
  (473 shorter events, 356.6 us)
Async XLA Ops:
  6.5 498.4 %copy-start = (bf16[256,2048]{1,0:T(8,128)(2,1)S(1)}, bf16[256,2048]{1,0:T(8,128)(2,1)}, u32[]{:S(2)}) copy-start(bf16[256,2048]{1,0:T(8,128)(2,1)} %param.19) | copy-start | bytes 3145732
  6.5 99.0 %all-gather.9.cloned.1.call-start = ((), (), s32[]{:S(2)}) async-start(), calls=%async_computation.4 | async-start | bytes 4325376 | tf_op jit(solution)/shard_map/all_gather | solution.py:19
  6.7 12.0 %copy-start.3 = (f32[128,128]{0,1:T(8,128)}, f32[128,128]{0,1:T(8,128)S(1)}, u32[]{:S(2)}) copy-start(f32[128,128]{0,1:T(8,128)S(1)} %copy.30) | copy-start | bytes 196612
  18.7 5.3 copy-start.6
  18.7 6.4 %copy-start.1 = (bf16[512,2,128]{2,1,0:T(2,128)(2,1)S(1)}, bf16[512,2,128]{2,1,0:T(2,128)(2,1)}, u32[]{:S(2)}) copy-start(bf16[512,2,128]{2,1,0:T(2,128)(2,1)} %param.15) | copy-start | bytes 786436
  23.9 178.8 %all-gather.7.cloned.1.call-start = ((), (), s32[]{:S(2)}) async-start(), calls=%async_computation.2 | async-start | bytes 8650752 | tf_op jit(solution)/shard_map/all_gather | solution.py:149
  24.8 276.0 %all-gather.5.cloned.1.call-start = ((), (), s32[]{:S(2)}) async-start(), calls=%async_computation.1 | async-start | bytes 8650752 | tf_op jit(solution)/shard_map/all_gather | solution.py:148
  25.1 2.9 copy-start.5
  25.1 80.5 %copy-start.4 = (f32[128,128]{0,1:T(8,128)S(1)}, f32[128,128]{0,1:T(8,128)}, u32[]{:S(2)}) copy-start(f32[128,128]{0,1:T(8,128)} %copy-done.3) | copy-start | bytes 196612
  147.4 4.8 copy-start.2
  150.4 415.4 %reduce-scatter.2.cloned.1.call-start = ((), (), s32[]{:S(2)}) async-start(), calls=%async_computation.3 | async-start | bytes 4718592 | tf_op jit(solution)/shard_map/reduce_scatter | solution.py:182
Sparse Core Ops, SparseCore 0:
  24.1 81.4 all-gather.8
  108.2 94.5 all-gather.6
  205.4 95.3 all-gather.4
  507.8 58.0 reduce-scatter.1
where the time goes:
time: 581 us; the launch traced here: 574 us
  waiting for transfers between devices  280 us (48%)
  matrix products  171 us (29%)
  other arithmetic  52 us (9%)
  local copies, waits for them, and re-layouts  51.8 us (9%)
  between operations  13.5 us (2%)
    all_gather x1, waiting for transfers between devices, on_device(): keys_all = lax.all_gather(rotated_key, 'seq', axis=0, tiled=True)  98 us
    all_gather x1, waiting for transfers between devices, carried_in(): pieces = lax.all_gather(value, axis)  77.6 us
    dot_general x29, matrix products, attend_update(): jnp.einsum('hqk,khd->hqd', weights.astype(jnp.bfloat16), values_part, pre...  59.6 us
    reduce_scatter x1, waiting for transfers between devices, on_device(): lax.psum_scatter(head_terms, 'head', scatter_dimension=1, tiled=True)  58.2 us
    all_gather x1, waiting for transfers between devices, on_device(): values_all = lax.all_gather(value, 'seq', axis=0, tiled=True)  46.3 us
    dot_general x29, matrix products, attend_update(): jnp.einsum('hqd,khd->hqk', queries, keys_part, preferred_element_type=jnp...  45.9 us
    dot_general x35, matrix products, chain_product(): return jnp.einsum('hij,hjk->hik', earlier, later, precision=HIGH)  41.9 us
    reshape x29, local copies, waits for them, and re-layouts, attend_update(): block_full = jnp.broadcast_to(block_part[:, :, None, :, None] == 1, (head...  34.2 us
  transfers between devices with their start and end apart: 4, of which 4 were waited for; matrix products, arithmetic and copies ran while one was open for 9% of the time, Pallas kernels for 0%

commit v1 on v0

v1 whole, which is shorter than its diff:
```python
from functools import partial
import math

import jax
import jax.numpy as jnp
from jax import lax
from jax.experimental import pallas as pl
from jax.experimental.pallas import tpu as pltpu
from jax.sharding import PartitionSpec as P

BLK = 128
DH = 128
XN = 4
ZN = 8
HL = 2
NB = 4
EPSILON = 1e-06
LOW = -1e30
SCALE = math.log2(math.e) / math.sqrt(DH)
f32 = jnp.float32
bf16 = jnp.bfloat16
NN = ((1,), (0,))
NT = ((1,), (1,))
TN = ((0,), (0,))
VMEM = pl.BlockSpec(memory_space=pltpu.VMEM)
SMEM = pl.BlockSpec(memory_space=pltpu.SMEM)


def params():
    return pltpu.CompilerParams(vmem_limit_bytes=48 * 1024 * 1024)


def dot1(a, b, dims=NN):
    return lax.dot_general(a, b, (dims, ((), ())), preferred_element_type=f32)


def halves(a):
    high = a.astype(bf16)
    return high, (a - high.astype(f32)).astype(bf16)


def dot3(a, b, dims=NN):
    ah, al = halves(a)
    bh, bl = halves(b)
    return dot1(ah, bh, dims) + (dot1(al, bh, dims) + dot1(ah, bl, dims))


def eye():
    row = lax.broadcasted_iota(jnp.int32, (BLK, BLK), 0)
    col = lax.broadcasted_iota(jnp.int32, (BLK, BLK), 1)
    return jnp.where(row == col, 1.0, 0.0).astype(f32)


def unit_rows(values):
    values = values.astype(f32)
    return values * lax.rsqrt(jnp.sum(values * values, axis=-1, keepdims=True) + EPSILON)


def factor_kernel(reflect_ref, tri_ref, frames_ref, total_ref):
    row = lax.broadcasted_iota(jnp.int32, (BLK, BLK), 0)
    col = lax.broadcasted_iota(jnp.int32, (BLK, BLK), 1)
    ident = jnp.where(row == col, 1.0, 0.0).astype(f32)
    items = [(h, b) for h in range(HL) for b in range(NB)]
    units = [unit_rows(reflect_ref[h, pl.ds(b * BLK, BLK), :]) for h, b in items]
    grams = [2.0 * dot3(u, u, NT) for u in units]
    inv = [ident - jnp.where((row // 2 == col // 2) & (row < col), g, 0.0) for g in grams]
    size = 2
    while size < BLK:
        off = (row // (2 * size) == col // (2 * size)) & (row // size < col // size)
        mids = [dot3(x, jnp.where(off, g, 0.0)) for x, g in zip(inv, grams)]
        inv = [x - dot3(m, x) for x, m in zip(inv, mids)]
        size *= 2
    wholes = []
    for (h, b), u, x in zip(items, units, inv):
        tri = 2.0 * x
        tri_ref[h, b] = tri
        wholes.append(ident - dot3(u, dot3(tri, u), TN))
    frames = [wholes[h * NB] for h in range(HL)]
    for b in range(1, NB):
        for h in range(HL):
            frames_ref[h, b - 1] = frames[h]
        frames = [dot3(frames[h], wholes[h * NB + b]) for h in range(HL)]
    for h in range(HL):
        total_ref[h] = frames[h]


def local_kernel(query_ref, key_ref, reflect_ref, tri_ref, frames_ref, qt_ref, k_ref):
    row = lax.broadcasted_iota(jnp.int32, (2 * BLK, BLK), 0) % BLK
    col = lax.broadcasted_iota(jnp.int32, (2 * BLK, BLK), 1)
    lower = col <= row
    for h in range(HL):
        for b in range(NB):
            here = pl.ds(b * BLK, BLK)
            unit = unit_rows(reflect_ref[h, here, :])
            uh, ul = halves(unit)
            both = jnp.concatenate([query_ref[h, here, :], key_ref[h, here, :]], axis=0)
            proj = dot1(both, uh, NT) + dot1(both, ul, NT)
            coef = dot3(jnp.where(lower, proj, 0.0), tri_ref[h, b], NT)
            turned = both.astype(f32) - dot3(coef, unit)
            if b > 0:
                turned = dot3(turned, frames_ref[h, b - 1], NT)
            qt_ref[h, b] = turned[:BLK].T
            k_ref[h, b] = turned[BLK:]


def row_kernel(where_ref, own_ref, one_ref, two_ref, three_ref, before_ref, total_ref):
    x = where_ref[1]
    for h in range(HL):
        cands = [own_ref[h], one_ref[h], two_ref[h], three_ref[h]]

        def pick(i):
            out = cands[0]
            for k in range(1, XN):
                out = jnp.where((x - k) % XN == i, cands[k], out)
            return out

        first = pick(0)
        second = dot3(first, pick(1))
        third = dot3(second, pick(2))
        before = jnp.where(x == 0, eye(), first)
        before = jnp.where(x == 2, second, before)
        before_ref[h] = jnp.where(x == 3, third, before)
        total_ref[h] = dot3(third, pick(3))


def hop_kernel(step, where_ref, left_ref, total_ref, before_ref, total_out, before_out):
    z = where_ref[0]
    for h in range(HL):
        left = jnp.where(z >= step, left_ref[h], eye())
        total_out[h] = dot3(left, total_ref[h])
        before_out[h] = dot3(left, before_ref[h])


def turn_kernel(where_ref, left_ref, before_ref, qt_ref, k_ref, qt_out, k_out):
    z = where_ref[0]
    for h in range(HL):
        left = jnp.where(z >= 4, left_ref[h], eye())
        frame = dot3(left, before_ref[h])
        for b in range(NB):
            qt_out[h, b] = dot3(frame, qt_ref[h, b]).astype(bf16)
            k_out[h, b] = dot3(k_ref[h, b], frame, NT).astype(bf16)


def attend_kernel(where_ref, count_ref, list_ref, *refs):
    queries = refs[:XN]
    keys = refs[XN : XN + ZN]
    values_ref = refs[XN + ZN]
    out_ref, lse_ref = refs[XN + ZN + 1 : XN + ZN + 3]
    scratch = refs[XN + ZN + 3 :]
    k_s, bias_s = scratch[0], scratch[1]
    q_s = scratch[2 : 2 + XN]
    m_s = scratch[2 + XN : 2 + 2 * XN]
    l_s = scratch[2 + 2 * XN : 2 + 3 * XN]
    acc_s = scratch[2 + 3 * XN : 2 + 4 * XN]
    z = where_ref[0]
    for j in range(ZN):
        source = (z - j + ZN) % ZN
        k_s[source] = keys[j][...]
    krow = lax.broadcasted_iota(jnp.int32, (BLK, BLK), 0)
    qcol = lax.broadcasted_iota(jnp.int32, (BLK, BLK), 1)
    bias_s[0] = jnp.zeros((BLK, BLK), f32)
    bias_s[1] = jnp.where(krow <= qcol, 0.0, LOW).astype(f32)
    bias_s[2] = jnp.full((BLK, BLK), LOW, f32)
    for a in range(XN):
        for h in range(HL):
            for i in range(NB):
                q_s[a][h * NB + i] = queries[a][h, i]
        q_s[a][HL * NB] = jnp.zeros((DH, BLK), bf16)
        m_s[a][...] = jnp.full(m_s[a].shape, LOW, f32)
        l_s[a][...] = jnp.zeros(l_s[a].shape, f32)
        acc_s[a][...] = jnp.zeros(acc_s[a].shape, f32)

    def step(t, carry):
        for a in range(XN):
            code = list_ref[a, t]
            qi = code & 15
            h = (code >> 2) & 1
            z1, j1 = (code >> 6) & 7, (code >> 4) & 3
            z2, j2 = (code >> 11) & 7, (code >> 9) & 3
            b1 = (code >> 14) & 3
            b2 = (code >> 16) & 3
            qt = q_s[a][qi]
            s1 = dot1(k_s[z1, h, j1], qt) + bias_s[b1]
            s2 = dot1(k_s[z2, h, j2], qt) + bias_s[b2]
            top = jnp.max(jnp.maximum(s1, s2), axis=0, keepdims=True) * SCALE
            m_old = m_s[a][qi]
            m_new = jnp.maximum(m_old, top)
            alpha = jnp.exp2(m_old - m_new)
            m_row = m_new[:1]
            p1 = jnp.exp2(s1 * SCALE - m_row)
            p2 = jnp.exp2(s2 * SCALE - m_row)
            l_s[a][qi] = l_s[a][qi] * alpha + jnp.sum(p1 + p2, axis=0, keepdims=True)
            m_s[a][qi] = m_new
            pt = jnp.concatenate([p1.astype(bf16), p2.astype(bf16)], axis=0)
            vt = jnp.concatenate([values_ref[z1, h, j1], values_ref[z2, h, j2]], axis=1)
            acc_s[a][qi] = acc_s[a][qi] * alpha[:1] + dot1(vt, pt)
        return carry

    most = count_ref[0]
    for a in range(1, XN):
        most = jnp.maximum(most, count_ref[a])
    lax.fori_loop(0, most, step, 0)
    for a in range(XN):
        for n in range(HL * NB):
            total = l_s[a][n][:1]
            some = total > 0.0
            safe = jnp.where(some, total, 1.0)
            out_ref[a, n] = (acc_s[a][n] * (1.0 / safe)).astype(bf16)
            lse_ref[a, pl.ds(n, 1), :] = jnp.where(some, m_s[a][n][:1] + jnp.log2(safe), LOW)


def project_kernel(*refs):
    parts = refs[:XN]
    lses = refs[XN : 2 * XN]
    weight_ref = refs[2 * XN]
    out_ref = refs[2 * XN + 1]
    for i in range(NB):
        mixed = []
        for h in range(HL):
            n = h * NB + i
            rows = [lse[pl.ds(n, 1), :] for lse in lses]
            top = jnp.maximum(jnp.maximum(rows[0], rows[1]), jnp.maximum(rows[2], rows[3]))
            shares = [jnp.exp2(r - top) for r in rows]
            scale = 1.0 / (shares[0] + shares[1] + shares[2] + shares[3])
            acc = parts[0][n].astype(f32) * (shares[0] * scale)
            for part, share in zip(parts[1:], shares[1:]):
                acc = acc + part[n].astype(f32) * (share * scale)
            mixed.append(acc.astype(bf16))
        rows = jnp.concatenate(mixed, axis=0).T
        for c in range(0, weight_ref.shape[1], 512):
            out_ref[pl.ds(i * BLK, BLK), pl.ds(c, 512)] = dot1(
                rows, weight_ref[:, pl.ds(c, 512)]
            ).astype(bf16)


def call(kernel, outs, ins, scratch=(), smem=0, flops=1e9):
    size = sum(math.prod(a.shape) * a.dtype.itemsize for a in ins)
    return pl.pallas_call(
        kernel,
        out_shape=outs,
        in_specs=[SMEM] * smem + [VMEM] * (len(ins) - smem),
        out_specs=jax.tree.map(lambda _: VMEM, outs),
        scratch_shapes=list(scratch),
        compiler_params=params(),
        cost_estimate=pl.CostEstimate(flops=int(flops), bytes_accessed=size, transcendentals=0),
    )(*ins)


def shape(*dims, dtype=f32):
    return jax.ShapeDtypeStruct(dims, dtype)


def work_lists(block_mask, z, x):
    heads = lax.broadcasted_iota(jnp.int32, (HL, XN, NB, ZN * NB), 1)
    lane_x = (x - heads + XN) % XN
    qpos = (z * XN + lane_x) * NB + lax.broadcasted_iota(jnp.int32, heads.shape, 2)
    kk = lax.broadcasted_iota(jnp.int32, heads.shape, 3)
    kpos = ((kk // NB) * XN + x) * NB + kk % NB
    rows = lax.dynamic_slice_in_dim(block_mask, z * XN * NB, XN * NB, 1)
    rows = rows.reshape(HL, XN, NB, ZN, XN, NB)
    rows = lax.dynamic_index_in_dim(rows, x, 4, keepdims=False).reshape(HL, XN, NB, ZN * NB)
    lanes = jnp.stack(
        [lax.dynamic_index_in_dim(rows, (x - a + XN) % XN, 1, keepdims=False) for a in range(XN)], 1
    )
    allowed = (lanes == 1) & (kpos <= qpos)
    flag = allowed.astype(jnp.int32)
    entry = kk + ZN * NB * jnp.where(kpos == qpos, 1, 0)
    before = jnp.sum(
        jnp.where(jnp.arange(ZN * NB)[:, None] < jnp.arange(ZN * NB)[None, :], flag[..., :, None], 0), -2
    )
    slot = jnp.where(allowed, before, -1)
    hit = slot[..., :, None] == jnp.arange(ZN * NB)[None, :]
    found = jnp.sum(hit.astype(jnp.int32), -2)
    ordered = jnp.sum(jnp.where(hit, entry[..., :, None], 0), -2)
    ordered = jnp.where(found > 0, ordered, 2 * ZN * NB)
    pairs = ordered.reshape(HL, XN, NB, ZN * NB // 2, 2)
    first, second = pairs[..., 0], pairs[..., 1]
    valid = found.reshape(HL, XN, NB, ZN * NB // 2, 2)[..., 0]
    qi = (
        lax.broadcasted_iota(jnp.int32, valid.shape, 0) * NB
        + lax.broadcasted_iota(jnp.int32, valid.shape, 2)
    )
    span = ZN * NB
    code = (
        qi
        + ((first % span) << 4)
        + ((second % span) << 9)
        + ((first // span) << 14)
        + ((second // span) << 16)
    )
    code = code.transpose(1, 0, 2, 3).reshape(XN, -1)
    valid = valid.transpose(1, 0, 2, 3).reshape(XN, -1)
    many = code.shape[1]
    place = jnp.sum(
        jnp.where(jnp.arange(many)[:, None] < jnp.arange(many)[None, :], valid[..., :, None], 0), -2
    )
    place = jnp.where(valid > 0, place, -1)
    put = place[..., :, None] == jnp.arange(many)[None, :]
    filled = jnp.sum(put.astype(jnp.int32), -2)
    lists = jnp.sum(jnp.where(put, code[..., :, None], 0), -2)
    dummy = HL * NB + (2 << 16)
    lists = jnp.where(filled > 0, lists, dummy)
    return jnp.sum(valid, -1), lists


def along_z(value, step):
    pairs = [(z * XN + x, ((z + step) % ZN) * XN + x) for z in range(ZN) for x in range(XN)]
    return lax.ppermute(value, "seq", pairs)


def up_z(value, step):
    pairs = [(z * XN + x, (z + step) * XN + x) for z in range(ZN - step) for x in range(XN)]
    return lax.ppermute(value, "seq", pairs)


def along_x(value, step):
    pairs = [(z * XN + x, z * XN + (x + step) % XN) for z in range(ZN) for x in range(XN)]
    return lax.ppermute(value, "seq", pairs)


def on_device(query, key, value, reflect, block_mask, out_weight):
    here = lax.axis_index("seq")
    z, x = here // XN, here % XN
    where = jnp.stack([z, x]).astype(jnp.int32)
    columns = [[z * XN + x for z in range(ZN)] for x in range(XN)]
    reflect_h = reflect.transpose(1, 0, 2)
    values_t = value.reshape(NB, BLK, HL, DH).transpose(2, 0, 3, 1)
    values_all = lax.all_gather(values_t, "seq", axis=0, axis_index_groups=columns)
    square = shape(HL, DH, DH)
    blocks = shape(HL, NB, BLK, DH)
    tri, frames, total = call(
        factor_kernel, (blocks, shape(HL, NB - 1, DH, DH), square), (reflect_h,), flops=2e9
    )
    others = [along_x(total, k) for k in range(1, XN)]
    q_local, k_local = call(
        local_kernel,
        (blocks, blocks),
        (query.transpose(1, 0, 2), key.transpose(1, 0, 2), reflect_h, tri, frames),
        flops=2e9,
    )
    counts, lists = work_lists(block_mask, z, x)
    before, total = call(row_kernel, (square, square), (where, total, *others), smem=1)
    for step in (1, 2):
        left = up_z(total, step)
        total, before = call(
            partial(hop_kernel, step), (square, square), (where, left, total, before), smem=1
        )
    left = up_z(total, 4)
    q_turned, k_turned = call(
        turn_kernel,
        (shape(HL, NB, DH, BLK, dtype=bf16), shape(HL, NB, BLK, DH, dtype=bf16)),
        (where, left, before, q_local, k_local),
        smem=1,
    )
    lanes = [q_turned] + [along_x(q_turned, k) for k in range(1, XN)]
    rows = [None] * ZN
    rows[0] = k_turned
    for j in range(1, 5):
        rows[j] = along_z(rows[j - 1], 1)
    for j in range(1, 4):
        rows[ZN - j] = along_z(rows[(ZN - j + 1) % ZN], -1)
    state = HL * NB + 1
    parts, lse = call(
        attend_kernel,
        (shape(XN, HL * NB, DH, BLK, dtype=bf16), shape(XN, HL * NB, BLK)),
        (where, counts, lists, *lanes, *rows, values_all),
        scratch=[pltpu.VMEM((ZN, HL, NB, BLK, DH), bf16), pltpu.VMEM((3, BLK, BLK), f32)]
        + [pltpu.VMEM((state, DH, BLK), bf16)] * XN
        + [pltpu.VMEM((state, 8, BLK), f32)] * XN
        + [pltpu.VMEM((state, 8, BLK), f32)] * XN
        + [pltpu.VMEM((state, DH, BLK), f32)] * XN,
        smem=3,
        flops=2e10,
    )
    got = [parts[0]] + [along_x(parts[a], -a) for a in range(1, XN)]
    got_lse = [lse[0]] + [along_x(lse[a], -a) for a in range(1, XN)]
    terms = call(
        project_kernel,
        shape(NB * BLK, out_weight.shape[1], dtype=bf16),
        (*got, *got_lse, out_weight),
    )
    return lax.psum_scatter(terms, "head", scatter_dimension=1, tiled=True)


def solution(mesh):
    in_specs = (
        P("seq", "head", None),
        P("seq", "head", None),
        P("seq", "head", None),
        P("seq", "head", None),
        P("head", None, None),
        P("head", None),
    )
    out_specs = P("seq", "head")
    return jax.shard_map(
        on_device, mesh=mesh, in_specs=in_specs, out_specs=out_specs, check_vma=False
    )
```

time: 581 us -> 202 us (0.35)
  waiting for transfers between devices: 280 us -> 102 us
  matrix products: 171 us -> 0 us
  other arithmetic: 52 us -> 1.78 us
  Pallas kernels: 0 us -> 48.6 us
  local copies, waits for them, and re-layouts: 51.8 us -> 4.08 us
  starting transfers between devices: 0.31 us -> 28.9 us
    all_gather x3 -> x1, waiting for transfers between devices: 222 us -> 0.01 us  [on_device(): lax.all_gather(values_t, 'seq', axis=0, axis_index_groups=columns)]
    dot_general x118 -> x0, matrix products: 171 us -> none  [the longest x29 59.6 us: attend_update(): jnp.einsum('hqk,khd->hqd', weights.astype(jnp.bfloat16), values_part, pre...]
    ppermute x0 -> x22, waiting for transfers between devices: none -> 58.3 us  [the longest x3 26.8 us: up_z(): return lax.ppermute(value, 'seq', pairs)]
    pallas_call x0 -> x8, Pallas kernels: none -> 48.6 us  [call(): pl.pallas_call(kernel, out_shape=outs, in_specs=[SMEM] * smem + [VMEM] *...]
    reshape x29 -> x3, local copies, waits for them, and re-layouts: 34.2 us -> 0.87 us  [the longest x1 0.68 us: work_lists(): rows = rows.reshape(HL, XN, NB, ZN, XN, NB)]
    ppermute x0 -> x22, starting transfers between devices: none -> 28.9 us  [the longest x12 13.1 us: along_x(): return lax.ppermute(value, 'seq', pairs)]
    eq x29 -> x0, other arithmetic: 23.4 us -> none  [attend_update(): block_part[:, :, None, :, None] == 1]
    reduce_sum x30 -> x4, other arithmetic: 19.7 us -> 0.98 us  [the longest x1 0.39 us: work_lists(): ordered = jnp.sum(jnp.where(hit, entry[..., :, None], 0), -2)]
  transfers between devices with their start and end apart: 4 -> 24, of which waited for: 4 -> 14; matrix products, arithmetic and copies ran while one was open for 9% -> 2% of each run, Pallas kernels for 0% -> 4%
where the time goes in v1:
time: 202 us; the launch traced here: 199 us
  waiting for transfers between devices  102 us (50%)
  Pallas kernels  48.6 us (24%)
  starting transfers between devices  28.9 us (14%)
  between operations  13.9 us (7%)
  local copies, waits for them, and re-layouts  4.08 us (2%)
    pallas_call x8, Pallas kernels, call(): pl.pallas_call(kernel, out_shape=outs, in_specs=[SMEM] * smem + [VMEM] *...  48.6 us
    reduce_scatter x1, waiting for transfers between devices, on_device(): return lax.psum_scatter(terms, 'head', scatter_dimension=1, tiled=True)  43.9 us
    ppermute x3, waiting for transfers between devices, up_z(): return lax.ppermute(value, 'seq', pairs)  26.8 us
    ppermute x7, waiting for transfers between devices, along_z(): return lax.ppermute(value, 'seq', pairs)  18.7 us
    ppermute x12, starting transfers between devices, along_x(): return lax.ppermute(value, 'seq', pairs)  13.1 us
    ppermute x12, waiting for transfers between devices, along_x(): return lax.ppermute(value, 'seq', pairs)  12.7 us
    ppermute x7, starting transfers between devices, along_z(): return lax.ppermute(value, 'seq', pairs)  11.8 us
    ppermute x3, starting transfers between devices, up_z(): return lax.ppermute(value, 'seq', pairs)  4.06 us
  transfers between devices with their start and end apart: 24, of which 14 were waited for; matrix products, arithmetic and copies ran while one was open for 2% of the time, Pallas kernels for 4%

profile of v1, /device:TPU:224, one launch (start us, length us, event | category | flops | bytes accessed | tf_op | source)
XLA Modules:
  0.0 199.5 jit_solution(6995207776078298240)
XLA Ops:
  7.6 4.2 %shard_map.64 = (f32[2,4,128,128]{3,2,1,0:T(8,128)S(1)}, f32[2,3,128,128]{3,2,1,0:T(8,128)S(1)}, f32[2,128,128]{2,1,0:T(8,128)S(1)}) custom-call(bf16[2,512,128]{2,1,0:T(8,128)(2,1)S(1)} %bitcast.42), custom_call_target="tpu_custom_call" | custom-call | flops 2000000000 | bytes 262144 | tf_op jit(solution)/shard_map/pallas_call | solution.py:238
  11.8 2.8 %collective-permute-start.2 = (f32[2,128,128]{2,1,0:T(8,128)S(1)}, f32[2,128,128]{2,1,0:T(8,128)S(1)}, u32[]{:S(2)}, u32[]{:S(2)}) collective-permute-start(f32[2,128,128]{2,1,0:T(8,128)S(1)} %get-tuple-element.20.own_ref), channel_id=1, source_target_pairs={{0,24},{8,0},{16,8},{24,16},{32,56},{40,32},{48,40},{56,48},{64,88... | collective-permute-start | bytes 393224 | tf_op jit(solution)/shard_map/ppermute | solution.py:318
  20.3 2.3 %collective-permute-done.1.two_ref = f32[2,128,128]{2,1,0:T(8,128)S(1)} collective-permute-done((f32[2,128,128]{2,1,0:T(8,128)S(1)}, f32[2,128,128]{2,1,0:T(8,128)S(1)}, u32[]{:S(2)}, u32[]{:S(2)}) %collective-permute-start.1) | collective-permute-done | bytes 131104 | tf_op jit(solution)/shard_map/ppermute | solution.py:318
  26.6 8.6 %collective-permute-done.3.left_ref = f32[2,128,128]{2,1,0:T(8,128)S(1)} collective-permute-done((f32[2,128,128]{2,1,0:T(8,128)S(1)}, f32[2,128,128]{2,1,0:T(8,128)S(1)}, u32[]{:S(2)}, u32[]{:S(2)}) %collective-permute-start.3) | collective-permute-done | bytes 131104 | tf_op jit(solution)/shard_map/ppermute | solution.py:313
  37.5 11.6 %collective-permute-done.4.left_ref = f32[2,128,128]{2,1,0:T(8,128)S(1)} collective-permute-done((f32[2,128,128]{2,1,0:T(8,128)S(1)}, f32[2,128,128]{2,1,0:T(8,128)S(1)}, u32[]{:S(2)}, u32[]{:S(2)}) %collective-permute-start.4) | collective-permute-done | bytes 131104 | tf_op jit(solution)/shard_map/ppermute | solution.py:313
  49.9 1.5 collective-permute-start.5
  51.4 3.8 %shard_map.68 = (f32[2,4,128,128]{3,2,1,0:T(8,128)S(1)}, f32[2,4,128,128]{3,2,1,0:T(8,128)S(1)}) custom-call(bf16[2,512,128]{2,1,0:T(8,128)(2,1)S(1)} %get-tuple-element.66.query_ref, bf16[2,512,128]{2,1,0:T(8,128)(2,1)S(1)} %get-tuple-element.65.key_ref, bf16[2,512,128]{2,1,0:T(8,128)(2,1)S(1)} %bitcast.43, ...), custom_call_target="tpu_custom_call" | custom-call | flops 2000000000 | bytes 1703936 | tf_op jit(solution)/shard_map/pallas_call | solution.py:238
  55.2 6.6 %collective-permute-done.5.left_ref = f32[2,128,128]{2,1,0:T(8,128)S(1)} collective-permute-done((f32[2,128,128]{2,1,0:T(8,128)S(1)}, f32[2,128,128]{2,1,0:T(8,128)S(1)}, u32[]{:S(2)}, u32[]{:S(2)}) %collective-permute-start.5) | collective-permute-done | bytes 131104 | tf_op jit(solution)/shard_map/ppermute | solution.py:313
  61.8 1.7 shard_map.69
  65.0 2.9 %collective-permute-start.13 = (bf16[2,4,128,128]{3,2,1,0:T(8,128)(2,1)S(1)}, bf16[2,4,128,128]{3,2,1,0:T(8,128)(2,1)S(1)}, u32[]{:S(2)}, u32[]{:S(2)}) collective-permute-start(bf16[2,4,128,128]{3,2,1,0:T(8,128)(2,1)S(1)} %get-tuple-element.32.refs_4_), channel_id=1, source_target_pairs={{0,224},{8,232},{16,240},{24,248},{32,0},{40,8},{48,16},{56,24},{6... | collective-permute-start | bytes 786440 | tf_op jit(solution)/shard_map/ppermute | solution.py:308
  67.9 6.8 %collective-permute-done.9.refs_5_ = bf16[2,4,128,128]{3,2,1,0:T(8,128)(2,1)S(1)} collective-permute-done((bf16[2,4,128,128]{3,2,1,0:T(8,128)(2,1)S(1)}, bf16[2,4,128,128]{3,2,1,0:T(8,128)(2,1)S(1)}, u32[]{:S(2)}, u32[]{:S(2)}) %collective-permute-start.9) | collective-permute-done | bytes 262176 | tf_op jit(solution)/shard_map/ppermute | solution.py:308
  75.0 2.2 %collective-permute-start.14 = (bf16[2,4,128,128]{3,2,1,0:T(8,128)(2,1)S(1)}, bf16[2,4,128,128]{3,2,1,0:T(8,128)(2,1)S(1)}, u32[]{:S(2)}, u32[]{:S(2)}) collective-permute-start(bf16[2,4,128,128]{3,2,1,0:T(8,128)(2,1)S(1)} %collective-permute-done.13.refs_11_), channel_id=1, source_target_pairs={{0,224},{8,232},{16,240},{24,248},{32,0},{40,8},{48,16},{56,24},{6... | collective-permute-start | bytes 786440 | tf_op jit(solution)/shard_map/ppermute | solution.py:308
  77.2 6.0 %collective-permute-done.10.refs_6_ = bf16[2,4,128,128]{3,2,1,0:T(8,128)(2,1)S(1)} collective-permute-done((bf16[2,4,128,128]{3,2,1,0:T(8,128)(2,1)S(1)}, bf16[2,4,128,128]{3,2,1,0:T(8,128)(2,1)S(1)}, u32[]{:S(2)}, u32[]{:S(2)}) %collective-permute-start.10) | collective-permute-done | bytes 262176 | tf_op jit(solution)/shard_map/ppermute | solution.py:308
  84.7 1.9 collective-permute-start.6
  87.7 3.2 %collective-permute-done.11.refs_7_ = bf16[2,4,128,128]{3,2,1,0:T(8,128)(2,1)S(1)} collective-permute-done((bf16[2,4,128,128]{3,2,1,0:T(8,128)(2,1)S(1)}, bf16[2,4,128,128]{3,2,1,0:T(8,128)(2,1)S(1)}, u32[]{:S(2)}, u32[]{:S(2)}) %collective-permute-start.11) | collective-permute-done | bytes 262176 | tf_op jit(solution)/shard_map/ppermute | solution.py:308
  90.9 3.3 %collective-permute-start.12 = (bf16[2,4,128,128]{3,2,1,0:T(8,128)(2,1)S(1)}, bf16[2,4,128,128]{3,2,1,0:T(8,128)(2,1)S(1)}, u32[]{:S(2)}, u32[]{:S(2)}) collective-permute-start(bf16[2,4,128,128]{3,2,1,0:T(8,128)(2,1)S(1)} %collective-permute-done.11.refs_7_), channel_id=1, source_target_pairs={{0,32},{8,40},{16,48},{24,56},{32,64},{40,72},{48,80},{56,88},{64,... | collective-permute-start | bytes 786440 | tf_op jit(solution)/shard_map/ppermute | solution.py:308
  95.4 2.7 %collective-permute-done.12.refs_8_ = bf16[2,4,128,128]{3,2,1,0:T(8,128)(2,1)S(1)} collective-permute-done((bf16[2,4,128,128]{3,2,1,0:T(8,128)(2,1)S(1)}, bf16[2,4,128,128]{3,2,1,0:T(8,128)(2,1)S(1)}, u32[]{:S(2)}, u32[]{:S(2)}) %collective-permute-start.12) | collective-permute-done | bytes 262176 | tf_op jit(solution)/shard_map/ppermute | solution.py:308
  98.1 33.9 %shard_map.70 = (bf16[4,8,128,128]{3,2,1,0:T(8,128)(2,1)S(1)}, f32[4,8,128]{2,1,0:T(8,128)S(1)}) custom-call(s32[2]{0:T(128)S(1)} %pad_add_fusion.where_ref, s32[4]{0:T(128)S(1)} %get-tuple-element.48.count_ref, s32[4,128]{1,0:T(4,128)S(1)} %compare_select_fusion.3.list_ref, bf16[2,4,128,128]{3,2,1,0:T(8,128)(2,1)S(1)} %get-tuple-element.31.refs_0_, ...), custom_call_target="tpu_custom_call" | custom-call | flops 20000000000 | bytes 5244952 | tf_op jit(solution)/shard_map/pallas_call | solution.py:238
  133.7 2.5 %collective-permute-start.16 = (bf16[8,128,128]{2,1,0:T(8,128)(2,1)S(1)}, bf16[8,128,128]{2,1,0:T(8,128)(2,1)S(1)}, u32[]{:S(2)}, u32[]{:S(2)}) collective-permute-start(bf16[8,128,128]{2,1,0:T(8,128)(2,1)S(1)} %get-tuple-element.43), channel_id=1, source_target_pairs={{0,24},{8,0},{16,8},{24,16},{32,56},{40,32},{48,40},{56,48},{64,88... | collective-permute-start | bytes 786440 | tf_op jit(solution)/shard_map/ppermute | solution.py:318
  136.5 2.1 %collective-permute-start.20 = (f32[8,128]{1,0:T(8,128)S(1)}, f32[8,128]{1,0:T(8,128)S(1)}, u32[]{:S(2)}, u32[]{:S(2)}) collective-permute-start(f32[8,128]{1,0:T(8,128)S(1)} %get-tuple-element.50), channel_id=1, source_target_pairs={{0,16},{8,24},{16,0},{24,8},{32,48},{40,56},{48,32},{56,40},{64,80... | collective-permute-start | bytes 12296 | tf_op jit(solution)/shard_map/ppermute | solution.py:318
  138.6 4.3 %collective-permute-done.21.refs_7_ = f32[8,128]{1,0:T(8,128)S(1)} collective-permute-done((f32[8,128]{1,0:T(8,128)S(1)}, f32[8,128]{1,0:T(8,128)S(1)}, u32[]{:S(2)}, u32[]{:S(2)}) %collective-permute-start.21) | collective-permute-done | bytes 4128 | tf_op jit(solution)/shard_map/ppermute | solution.py:318
  142.9 3.6 %collective-permute-done.19.refs_5_ = f32[8,128]{1,0:T(8,128)S(1)} collective-permute-done((f32[8,128]{1,0:T(8,128)S(1)}, f32[8,128]{1,0:T(8,128)S(1)}, u32[]{:S(2)}, u32[]{:S(2)}) %collective-permute-start.19) | collective-permute-done | bytes 4128 | tf_op jit(solution)/shard_map/ppermute | solution.py:318
  146.5 2.2 %shard_map.71 = bf16[512,2048]{1,0:T(8,128)(2,1)} custom-call(bf16[8,128,128]{2,1,0:T(8,128)(2,1)S(1)} %get-tuple-element.44.refs_0_, bf16[8,128,128]{2,1,0:T(8,128)(2,1)S(1)} %collective-permute-done.16.refs_1_, bf16[8,128,128]{2,1,0:T(8,128)(2,1)S(1)} %collective-permute-done.17.refs_2_, bf16[8,128,128]{2,1,0:T(8,128)(2,1)S(1)} %collective-permute-done.18.refs_3_, ...), custom_call_target="tpu_custom_call" | custom-call | flops 1000000000 | bytes 2113536 | tf_op jit(solution)/shard_map/pallas_call | solution.py:238
  148.7 43.9 %reduce-scatter.2.cloned.1.call-done = bf16[512,256]{1,0:T(8,128)(2,1)} async-done(((bf16[512,2048]{1,0:T(8,128)(2,1)}), bf16[512,256]{1,0:T(8,128)(2,1)}) %reduce-scatter.2.cloned.1.call-update) | async-done | bytes 262160 | tf_op jit(solution)/shard_map/reduce_scatter | solution.py:382
  (83 shorter events, 21.0 us)
Async XLA Ops:
  6.5 91.6 %all-gather.3.cloned.1.call-start = ((), (), s32[]{:S(2)}) async-start(), calls=%async_computation.2 | async-start | bytes 2359296 | tf_op jit(solution)/shard_map/all_gather | solution.py:328
  11.8 8.4 %collective-permute-start.2 = (f32[2,128,128]{2,1,0:T(8,128)S(1)}, f32[2,128,128]{2,1,0:T(8,128)S(1)}, u32[]{:S(2)}, u32[]{:S(2)}) collective-permute-start(f32[2,128,128]{2,1,0:T(8,128)S(1)} %get-tuple-element.20.own_ref), channel_id=1, source_target_pairs={{0,24},{8,0},{16,8},{24,16},{32,56},{40,32},{48,40},{56,48},{64,88... | collective-permute-start | bytes 393224 | tf_op jit(solution)/shard_map/ppermute | solution.py:318
  14.7 7.9 %collective-permute-start.1 = (f32[2,128,128]{2,1,0:T(8,128)S(1)}, f32[2,128,128]{2,1,0:T(8,128)S(1)}, u32[]{:S(2)}, u32[]{:S(2)}) collective-permute-start(f32[2,128,128]{2,1,0:T(8,128)S(1)} %get-tuple-element.20.own_ref), channel_id=1, source_target_pairs={{0,16},{8,24},{16,0},{24,8},{32,48},{40,56},{48,32},{56,40},{64,80... | collective-permute-start | bytes 393224 | tf_op jit(solution)/shard_map/ppermute | solution.py:318
  15.5 8.5 %collective-permute-start = (f32[2,128,128]{2,1,0:T(8,128)S(1)}, f32[2,128,128]{2,1,0:T(8,128)S(1)}, u32[]{:S(2)}, u32[]{:S(2)}) collective-permute-start(f32[2,128,128]{2,1,0:T(8,128)S(1)} %get-tuple-element.20.own_ref), channel_id=1, source_target_pairs={{0,8},{8,16},{16,24},{24,0},{32,40},{40,48},{48,56},{56,32},{64,72... | collective-permute-start | bytes 393224 | tf_op jit(solution)/shard_map/ppermute | solution.py:318
  17.3 175.4 %reduce-scatter.2.cloned.1.call-start = ((), (), s32[]{:S(2)}) async-start(), calls=%async_computation.1 | async-start | bytes 2359296 | tf_op jit(solution)/shard_map/reduce_scatter | solution.py:382
  25.2 10.0 %collective-permute-start.3 = (f32[2,128,128]{2,1,0:T(8,128)S(1)}, f32[2,128,128]{2,1,0:T(8,128)S(1)}, u32[]{:S(2)}, u32[]{:S(2)}) collective-permute-start(f32[2,128,128]{2,1,0:T(8,128)S(1)} %get-tuple-element.21.total_ref), channel_id=1, source_target_pairs={{0,32},{8,40},{16,48},{24,56},{32,64},{40,72},{48,80},{56,88},{64,... | collective-permute-start | bytes 393224 | tf_op jit(solution)/shard_map/ppermute | solution.py:313
  36.0 13.2 %collective-permute-start.4 = (f32[2,128,128]{2,1,0:T(8,128)S(1)}, f32[2,128,128]{2,1,0:T(8,128)S(1)}, u32[]{:S(2)}, u32[]{:S(2)}) collective-permute-start(f32[2,128,128]{2,1,0:T(8,128)S(1)} %get-tuple-element.23.total_ref), channel_id=1, source_target_pairs={{0,64},{8,72},{16,80},{24,88},{32,96},{40,104},{48,112},{56,120},{... | collective-permute-start | bytes 393224 | tf_op jit(solution)/shard_map/ppermute | solution.py:313
  49.9 11.9 %collective-permute-start.5 = (f32[2,128,128]{2,1,0:T(8,128)S(1)}, f32[2,128,128]{2,1,0:T(8,128)S(1)}, u32[]{:S(2)}, u32[]{:S(2)}) collective-permute-start(f32[2,128,128]{2,1,0:T(8,128)S(1)} %get-tuple-element.25), channel_id=1, source_target_pairs={{0,128},{8,136},{16,144},{24,152},{32,160},{40,168},{48,176},{56,1... | collective-permute-start | bytes 393224 | tf_op jit(solution)/shard_map/ppermute | solution.py:313
  63.5 11.1 %collective-permute-start.9 = (bf16[2,4,128,128]{3,2,1,0:T(8,128)(2,1)S(1)}, bf16[2,4,128,128]{3,2,1,0:T(8,128)(2,1)S(1)}, u32[]{:S(2)}, u32[]{:S(2)}) collective-permute-start(bf16[2,4,128,128]{3,2,1,0:T(8,128)(2,1)S(1)} %get-tuple-element.32.refs_4_), channel_id=1, source_target_pairs={{0,32},{8,40},{16,48},{24,56},{32,64},{40,72},{48,80},{56,88},{64,... | collective-permute-start | bytes 786440 | tf_op jit(solution)/shard_map/ppermute | solution.py:308
  65.0 10.0 %collective-permute-start.13 = (bf16[2,4,128,128]{3,2,1,0:T(8,128)(2,1)S(1)}, bf16[2,4,128,128]{3,2,1,0:T(8,128)(2,1)S(1)}, u32[]{:S(2)}, u32[]{:S(2)}) collective-permute-start(bf16[2,4,128,128]{3,2,1,0:T(8,128)(2,1)S(1)} %get-tuple-element.32.refs_4_), channel_id=1, source_target_pairs={{0,224},{8,232},{16,240},{24,248},{32,0},{40,8},{48,16},{56,24},{6... | collective-permute-start | bytes 786440 | tf_op jit(solution)/shard_map/ppermute | solution.py:308
  74.6 8.6 %collective-permute-start.10 = (bf16[2,4,128,128]{3,2,1,0:T(8,128)(2,1)S(1)}, bf16[2,4,128,128]{3,2,1,0:T(8,128)(2,1)S(1)}, u32[]{:S(2)}, u32[]{:S(2)}) collective-permute-start(bf16[2,4,128,128]{3,2,1,0:T(8,128)(2,1)S(1)} %collective-permute-done.9.refs_5_), channel_id=1, source_target_pairs={{0,32},{8,40},{16,48},{24,56},{32,64},{40,72},{48,80},{56,88},{64,... | collective-permute-start | bytes 786440 | tf_op jit(solution)/shard_map/ppermute | solution.py:308
  75.0 11.7 %collective-permute-start.14 = (bf16[2,4,128,128]{3,2,1,0:T(8,128)(2,1)S(1)}, bf16[2,4,128,128]{3,2,1,0:T(8,128)(2,1)S(1)}, u32[]{:S(2)}, u32[]{:S(2)}) collective-permute-start(bf16[2,4,128,128]{3,2,1,0:T(8,128)(2,1)S(1)} %collective-permute-done.13.refs_11_), channel_id=1, source_target_pairs={{0,224},{8,232},{16,240},{24,248},{32,0},{40,8},{48,16},{56,24},{6... | collective-permute-start | bytes 786440 | tf_op jit(solution)/shard_map/ppermute | solution.py:308
  83.2 7.7 %collective-permute-start.11 = (bf16[2,4,128,128]{3,2,1,0:T(8,128)(2,1)S(1)}, bf16[2,4,128,128]{3,2,1,0:T(8,128)(2,1)S(1)}, u32[]{:S(2)}, u32[]{:S(2)}) collective-permute-start(bf16[2,4,128,128]{3,2,1,0:T(8,128)(2,1)S(1)} %collective-permute-done.10.refs_6_), channel_id=1, source_target_pairs={{0,32},{8,40},{16,48},{24,56},{32,64},{40,72},{48,80},{56,88},{64,... | collective-permute-start | bytes 786440 | tf_op jit(solution)/shard_map/ppermute | solution.py:308
  84.5 9.9 %collective-permute-start.8 = (bf16[2,4,128,128]{3,2,1,0:T(8,128)(2,1)S(1)}, bf16[2,4,128,128]{3,2,1,0:T(8,128)(2,1)S(1)}, u32[]{:S(2)}, u32[]{:S(2)}) collective-permute-start(bf16[2,4,128,128]{3,2,1,0:T(8,128)(2,1)S(1)} %get-tuple-element.31.refs_0_), channel_id=1, source_target_pairs={{0,24},{8,0},{16,8},{24,16},{32,56},{40,32},{48,40},{56,48},{64,88... | collective-permute-start | bytes 786440 | tf_op jit(solution)/shard_map/ppermute | solution.py:318
  84.6 9.9 %collective-permute-start.7 = (bf16[2,4,128,128]{3,2,1,0:T(8,128)(2,1)S(1)}, bf16[2,4,128,128]{3,2,1,0:T(8,128)(2,1)S(1)}, u32[]{:S(2)}, u32[]{:S(2)}) collective-permute-start(bf16[2,4,128,128]{3,2,1,0:T(8,128)(2,1)S(1)} %get-tuple-element.31.refs_0_), channel_id=1, source_target_pairs={{0,16},{8,24},{16,0},{24,8},{32,48},{40,56},{48,32},{56,40},{64,80... | collective-permute-start | bytes 786440 | tf_op jit(solution)/shard_map/ppermute | solution.py:318
  84.7 10.7 %collective-permute-start.6 = (bf16[2,4,128,128]{3,2,1,0:T(8,128)(2,1)S(1)}, bf16[2,4,128,128]{3,2,1,0:T(8,128)(2,1)S(1)}, u32[]{:S(2)}, u32[]{:S(2)}) collective-permute-start(bf16[2,4,128,128]{3,2,1,0:T(8,128)(2,1)S(1)} %get-tuple-element.31.refs_0_), channel_id=1, source_target_pairs={{0,8},{8,16},{16,24},{24,0},{32,40},{40,48},{48,56},{56,32},{64,72... | collective-permute-start | bytes 786440 | tf_op jit(solution)/shard_map/ppermute | solution.py:318
  86.7 8.8 %collective-permute-start.15 = (bf16[2,4,128,128]{3,2,1,0:T(8,128)(2,1)S(1)}, bf16[2,4,128,128]{3,2,1,0:T(8,128)(2,1)S(1)}, u32[]{:S(2)}, u32[]{:S(2)}) collective-permute-start(bf16[2,4,128,128]{3,2,1,0:T(8,128)(2,1)S(1)} %collective-permute-done.14.refs_10_), channel_id=1, source_target_pairs={{0,224},{8,232},{16,240},{24,248},{32,0},{40,8},{48,16},{56,24},{6... | collective-permute-start | bytes 786440 | tf_op jit(solution)/shard_map/ppermute | solution.py:308
  90.9 7.2 %collective-permute-start.12 = (bf16[2,4,128,128]{3,2,1,0:T(8,128)(2,1)S(1)}, bf16[2,4,128,128]{3,2,1,0:T(8,128)(2,1)S(1)}, u32[]{:S(2)}, u32[]{:S(2)}) collective-permute-start(bf16[2,4,128,128]{3,2,1,0:T(8,128)(2,1)S(1)} %collective-permute-done.11.refs_7_), channel_id=1, source_target_pairs={{0,32},{8,40},{16,48},{24,56},{32,64},{40,72},{48,80},{56,88},{64,... | collective-permute-start | bytes 786440 | tf_op jit(solution)/shard_map/ppermute | solution.py:308
  132.1 14.4 %collective-permute-start.18 = (bf16[8,128,128]{2,1,0:T(8,128)(2,1)S(1)}, bf16[8,128,128]{2,1,0:T(8,128)(2,1)S(1)}, u32[]{:S(2)}, u32[]{:S(2)}) collective-permute-start(bf16[8,128,128]{2,1,0:T(8,128)(2,1)S(1)} %get-tuple-element.41), channel_id=1, source_target_pairs={{0,8},{8,16},{16,24},{24,0},{32,40},{40,48},{48,56},{56,32},{64,72... | collective-permute-start | bytes 786440 | tf_op jit(solution)/shard_map/ppermute | solution.py:318
  132.4 14.1 %collective-permute-start.17 = (bf16[8,128,128]{2,1,0:T(8,128)(2,1)S(1)}, bf16[8,128,128]{2,1,0:T(8,128)(2,1)S(1)}, u32[]{:S(2)}, u32[]{:S(2)}) collective-permute-start(bf16[8,128,128]{2,1,0:T(8,128)(2,1)S(1)} %get-tuple-element.42), channel_id=1, source_target_pairs={{0,16},{8,24},{16,0},{24,8},{32,48},{40,56},{48,32},{56,40},{64,80... | collective-permute-start | bytes 786440 | tf_op jit(solution)/shard_map/ppermute | solution.py:318
  133.7 12.8 %collective-permute-start.16 = (bf16[8,128,128]{2,1,0:T(8,128)(2,1)S(1)}, bf16[8,128,128]{2,1,0:T(8,128)(2,1)S(1)}, u32[]{:S(2)}, u32[]{:S(2)}) collective-permute-start(bf16[8,128,128]{2,1,0:T(8,128)(2,1)S(1)} %get-tuple-element.43), channel_id=1, source_target_pairs={{0,24},{8,0},{16,8},{24,16},{32,56},{40,32},{48,40},{56,48},{64,88... | collective-permute-start | bytes 786440 | tf_op jit(solution)/shard_map/ppermute | solution.py:318
  136.3 6.6 %collective-permute-start.21 = (f32[8,128]{1,0:T(8,128)S(1)}, f32[8,128]{1,0:T(8,128)S(1)}, u32[]{:S(2)}, u32[]{:S(2)}) collective-permute-start(f32[8,128]{1,0:T(8,128)S(1)} %get-tuple-element.49), channel_id=1, source_target_pairs={{0,8},{8,16},{16,24},{24,0},{32,40},{40,48},{48,56},{56,32},{64,72... | collective-permute-start | bytes 12296 | tf_op jit(solution)/shard_map/ppermute | solution.py:318
  136.5 6.4 %collective-permute-start.20 = (f32[8,128]{1,0:T(8,128)S(1)}, f32[8,128]{1,0:T(8,128)S(1)}, u32[]{:S(2)}, u32[]{:S(2)}) collective-permute-start(f32[8,128]{1,0:T(8,128)S(1)} %get-tuple-element.50), channel_id=1, source_target_pairs={{0,16},{8,24},{16,0},{24,8},{32,48},{40,56},{48,32},{56,40},{64,80... | collective-permute-start | bytes 12296 | tf_op jit(solution)/shard_map/ppermute | solution.py:318
  142.9 3.6 %collective-permute-start.19 = (f32[8,128]{1,0:T(8,128)S(1)}, f32[8,128]{1,0:T(8,128)S(1)}, u32[]{:S(2)}, u32[]{:S(2)}) collective-permute-start(f32[8,128]{1,0:T(8,128)S(1)} %get-tuple-element.51), channel_id=1, source_target_pairs={{0,24},{8,0},{16,8},{24,16},{32,56},{40,32},{48,40},{56,48},{64,88... | collective-permute-start | bytes 12296 | tf_op jit(solution)/shard_map/ppermute | solution.py:318
  (5 other events, 49.1 us)
Sparse Core Ops, SparseCore 0:
  17.4 45.5 all-gather.2
  148.9 43.7 reduce-scatter.1

commit v2 on v1

v2 whole, which is shorter than its diff:
```python
from functools import partial
import math

import jax
import jax.numpy as jnp
from jax import lax
from jax.experimental import pallas as pl
from jax.experimental.pallas import tpu as pltpu
from jax.sharding import PartitionSpec as P

BLK = 128
DH = 128
XN = 4
ZN = 8
HL = 2
NB = 4
YN = 4
QB = HL * XN * NB
LANES = 8
LSE = 16
SLOTS = 256
CALLS = ((0,), (1, 7), (2, 6), (3, 5, 4))
EPSILON = 1e-06
LOW = -1e30
SCALE = math.log2(math.e) / math.sqrt(DH)
f32 = jnp.float32
bf16 = jnp.bfloat16
NN = ((1,), (0,))
NT = ((1,), (1,))
TN = ((0,), (0,))
VMEM = pl.BlockSpec(memory_space=pltpu.VMEM)
SMEM = pl.BlockSpec(memory_space=pltpu.SMEM)


def params(mib):
    return pltpu.CompilerParams(vmem_limit_bytes=mib * 1024 * 1024)


def dot1(a, b, dims=NN):
    return lax.dot_general(a, b, (dims, ((), ())), preferred_element_type=f32)


def halves(a):
    high = a.astype(bf16)
    return high, (a - high.astype(f32)).astype(bf16)


def dot3(a, b, dims=NN):
    ah, al = halves(a)
    bh, bl = halves(b)
    return dot1(ah, bh, dims) + (dot1(al, bh, dims) + dot1(ah, bl, dims))


def eye():
    row = lax.broadcasted_iota(jnp.int32, (BLK, BLK), 0)
    col = lax.broadcasted_iota(jnp.int32, (BLK, BLK), 1)
    return jnp.where(row == col, 1.0, 0.0).astype(f32)


def unit_rows(values):
    values = values.astype(f32)
    return values * lax.rsqrt(jnp.sum(values * values, axis=-1, keepdims=True) + EPSILON)


def factor_kernel(reflect_ref, tri_ref, frames_ref, total_ref):
    row = lax.broadcasted_iota(jnp.int32, (BLK, BLK), 0)
    col = lax.broadcasted_iota(jnp.int32, (BLK, BLK), 1)
    ident = jnp.where(row == col, 1.0, 0.0).astype(f32)
    items = [(h, b) for h in range(HL) for b in range(NB)]
    units = [unit_rows(reflect_ref[h, pl.ds(b * BLK, BLK), :]) for h, b in items]
    grams = [2.0 * dot3(u, u, NT) for u in units]
    inv = [ident - jnp.where((row // 2 == col // 2) & (row < col), g, 0.0) for g in grams]
    size = 2
    while size < BLK:
        off = (row // (2 * size) == col // (2 * size)) & (row // size < col // size)
        mids = [dot3(x, jnp.where(off, g, 0.0)) for x, g in zip(inv, grams)]
        inv = [x - dot3(m, x) for x, m in zip(inv, mids)]
        size *= 2
    wholes = []
    for (h, b), u, x in zip(items, units, inv):
        tri = 2.0 * x
        tri_ref[h, b] = tri
        wholes.append(ident - dot3(u, dot3(tri, u), TN))
    frames = [wholes[h * NB] for h in range(HL)]
    for b in range(1, NB):
        for h in range(HL):
            frames_ref[h, b - 1] = frames[h]
        frames = [dot3(frames[h], wholes[h * NB + b]) for h in range(HL)]
    for h in range(HL):
        total_ref[h] = frames[h]


def local_kernel(query_ref, key_ref, reflect_ref, tri_ref, frames_ref, qt_ref, k_ref):
    row = lax.broadcasted_iota(jnp.int32, (2 * BLK, BLK), 0) % BLK
    col = lax.broadcasted_iota(jnp.int32, (2 * BLK, BLK), 1)
    lower = col <= row
    for h in range(HL):
        for b in range(NB):
            here = pl.ds(b * BLK, BLK)
            unit = unit_rows(reflect_ref[h, here, :])
            uh, ul = halves(unit)
            both = jnp.concatenate([query_ref[h, here, :], key_ref[h, here, :]], axis=0)
            proj = dot1(both, uh, NT) + dot1(both, ul, NT)
            coef = dot3(jnp.where(lower, proj, 0.0), tri_ref[h, b], NT)
            turned = both.astype(f32) - dot3(coef, unit)
            if b > 0:
                turned = dot3(turned, frames_ref[h, b - 1], NT)
            qt_ref[h, b] = turned[:BLK].T
            k_ref[h, b] = turned[BLK:]


def row_kernel(where_ref, own_ref, one_ref, two_ref, three_ref, before_ref, total_ref):
    x = where_ref[1]
    for h in range(HL):
        cands = [own_ref[h], one_ref[h], two_ref[h], three_ref[h]]

        def pick(i):
            out = cands[0]
            for k in range(1, XN):
                out = jnp.where((x - k + XN) % XN == i, cands[k], out)
            return out

        first = pick(0)
        second = dot3(first, pick(1))
        third = dot3(second, pick(2))
        for a in range(XN):
            lane = (x - a + XN) % XN
            before = jnp.where(lane == 0, eye(), first)
            before = jnp.where(lane == 2, second, before)
            before_ref[a, h] = jnp.where(lane == 3, third, before)
        total_ref[h] = dot3(third, pick(3))


def hop_kernel(step, where_ref, left_ref, total_ref, *refs):
    z = where_ref[0]
    total_out, chain_out = refs[-2:]
    for h in range(HL):
        left = jnp.where(z >= step, left_ref[h], eye())
        total_out[h] = dot3(left, total_ref[h])
        chain_out[h] = left if step == 1 else dot3(left, refs[0][h])


def turn_key_kernel(where_ref, left_ref, chain_ref, before_ref, k_ref, k_out, chain_out):
    z = where_ref[0]
    for h in range(HL):
        left = jnp.where(z >= 4, left_ref[h], eye())
        chain = dot3(left, chain_ref[h])
        chain_out[h] = chain
        frame = dot3(chain, before_ref[0, h])
        for b in range(NB):
            k_out[h, b] = dot3(k_ref[h, b], frame, NT).astype(bf16)


def turn_query_kernel(chain_ref, before_ref, *refs):
    lanes, out_ref = refs[:XN], refs[XN]
    for a in range(XN):
        for h in range(HL):
            frame = dot3(chain_ref[h], before_ref[a, h])
            for b in range(NB):
                out_ref[(h * XN + a) * NB + b] = dot3(frame, lanes[a][h, b]).astype(bf16)
    out_ref[QB] = jnp.zeros((DH, BLK), bf16)


def attend_kernel(index, first, last, rows, *refs):
    refs = list(refs)
    list_ref, q_ref = refs[:2]
    keys, values = refs[2 : 2 + rows], refs[2 + rows : 2 + 2 * rows]
    refs = refs[2 + 2 * rows :]
    carried = None
    if not first:
        carried, refs = refs[:3], refs[3:]
    if last:
        out_ref, m_s, l_s, acc_s, k_s, v_s, bias_s, p_s, a_s = refs
    else:
        m_s, l_s, acc_s, k_s, v_s, bias_s, p_s, a_s = refs
    for r in range(rows):
        k_s[r] = keys[r][...]
        v_s[r] = values[r][...]
    krow = lax.broadcasted_iota(jnp.int32, (BLK, BLK), 0)
    qcol = lax.broadcasted_iota(jnp.int32, (BLK, BLK), 1)
    bias_s[0] = jnp.zeros((BLK, BLK), f32)
    bias_s[1] = jnp.where(krow <= qcol, 0.0, LOW).astype(f32)
    bias_s[2] = jnp.full((BLK, BLK), LOW, f32)
    if first:
        m_s[...] = jnp.full(m_s.shape, LOW, f32)
        l_s[...] = jnp.zeros(l_s.shape, f32)
        acc_s[...] = jnp.zeros(acc_s.shape, f32)
    else:
        m_s[...] = carried[0][...]
        l_s[...] = carried[1][...]
        acc_s[...] = carried[2][...]
    p_s[...] = jnp.zeros(p_s.shape, bf16)
    a_s[...] = jnp.ones(a_s.shape, f32)
    group = range(LANES)

    def codes(t):
        out = []
        for a in group:
            code = list_ref[index, t * LANES + a]
            out.append(
                (
                    code & 63,
                    (code >> 4) & 1,
                    ((code >> 8) & 3, (code >> 6) & 3),
                    ((code >> 12) & 3, (code >> 10) & 3),
                    (code >> 14) & 3,
                    (code >> 16) & 3,
                )
            )
        return out

    def value_term(a, item):
        qi, h, k1, k2 = item[:4]
        vt = jnp.concatenate([v_s[k1[0], h, k1[1]], v_s[k2[0], h, k2[1]]], axis=1)
        return acc_s[qi] * a_s[a][:1] + dot1(vt, p_s[a])

    def step(t, carry):
        prev = codes(jnp.maximum(t - 1, 0))
        items = codes(t)
        m_old = [m_s[c[0]] for c in items]
        l_old = [l_s[c[0]] for c in items]

        def score(a):
            qi, h, k1, k2, b1, b2 = items[a]
            qt = q_ref[qi]
            return (
                dot1(k_s[k1[0], h, k1[1]], qt) + bias_s[b1],
                dot1(k_s[k2[0], h, k2[1]], qt) + bias_s[b2],
            )

        ahead = score(0)
        for a in group:
            s1, s2 = ahead
            if a + 1 < LANES:
                ahead = score(a + 1)
            acc = value_term(a, prev[a])
            top = jnp.max(jnp.maximum(s1, s2), axis=0, keepdims=True) * SCALE
            m = jnp.maximum(m_old[a], top)
            alpha = jnp.exp2(m_old[a] - m)
            p1 = jnp.exp2(s1 * SCALE - m[:1])
            p2 = jnp.exp2(s2 * SCALE - m[:1])
            acc_s[prev[a][0]] = acc
            m_s[items[a][0]] = m
            l_s[items[a][0]] = l_old[a] * alpha + jnp.sum(p1 + p2, axis=0, keepdims=True)
            a_s[a] = alpha
            p_s[a] = jnp.concatenate([p1.astype(bf16), p2.astype(bf16)], axis=0)
        return carry

    count = list_ref[index, SLOTS - 1]
    lax.fori_loop(0, count, step, 0)
    prev = codes(jnp.maximum(count - 1, 0))
    for a in group:
        acc_s[prev[a][0]] = value_term(a, prev[a])
    if last:
        sub = lax.broadcasted_iota(jnp.int32, (LSE, BLK), 0)
        for a in range(XN):
            for h in range(HL):
                for i in range(NB):
                    n = (h * XN + a) * NB + i
                    total = l_s[n][:1]
                    some = total > 0.0
                    safe = jnp.where(some, total, 1.0)
                    lse = jnp.where(some, m_s[n][:1] + jnp.log2(safe), LOW)
                    out_ref[a, h * NB + i, :DH] = (acc_s[n] * (1.0 / safe)).astype(bf16)
                    one = lse.astype(bf16).astype(f32)
                    two = (lse - one).astype(bf16).astype(f32)
                    three = (lse - one) - two
                    extra = jnp.where(sub == 0, one, jnp.where(sub == 1, two, jnp.where(sub == 2, three, 0.0)))
                    out_ref[a, h * NB + i, DH:] = extra.astype(bf16)


def combine_kernel(where_ref, *refs):
    parts, weight_ref, out_ref, mixed_ref = refs[:XN], refs[XN], refs[XN + 1], refs[XN + 2]
    y, core = where_ref[2], where_ref[3]
    for i in range(NB):
        mixed = []
        for h in range(HL):
            n = h * NB + i
            rows = []
            for part in parts:
                extra = part[n, DH:].astype(f32)
                rows.append(extra[:1] + extra[1:2] + extra[2:3])
            top = jnp.maximum(jnp.maximum(rows[0], rows[1]), jnp.maximum(rows[2], rows[3]))
            shares = [jnp.exp2(r - top) for r in rows]
            scale = 1.0 / (shares[0] + shares[1] + shares[2] + shares[3])
            acc = parts[0][n, :DH].astype(f32) * (shares[0] * scale)
            for part, share in zip(parts[1:], shares[1:]):
                acc = acc + part[n, :DH].astype(f32) * (share * scale)
            mixed.append(acc.astype(bf16))
        mixed_ref[pl.ds(i * BLK, BLK), :] = jnp.concatenate(mixed, axis=0).T
    for k in range(YN):
        block = weight_ref[((y + k) % YN) * 2 + 1 - core]
        out_ref[k] = dot1(mixed_ref[...], block).astype(bf16)


def own_terms_kernel(where_ref, mixed_ref, weight_ref, out_ref):
    y, core = where_ref[2], where_ref[3]
    for k in range(YN):
        out_ref[k] = dot1(mixed_ref[...], weight_ref[((y + k) % YN) * 2 + core])


def pair_sum_kernel(own_ref, other_ref, keep_ref, *send_refs):
    keep_ref[...] = own_ref[0] + other_ref[0].astype(f32)
    for k, send in enumerate(send_refs):
        send[...] = (own_ref[k + 1] + other_ref[k + 1].astype(f32)).astype(bf16)


def final_sum_kernel(keep_ref, one_ref, two_ref, three_ref, out_ref):
    total = keep_ref[...] + one_ref[...].astype(f32)
    out_ref[...] = (total + (two_ref[...].astype(f32) + three_ref[...].astype(f32))).astype(bf16)


def list_kernel(where_ref, mask_ref, out_ref):
    z, x = where_ref[0], where_ref[1]
    rows = [mask_ref[h, pl.ds(pl.multiple_of(z * XN * NB, XN * NB), XN * NB), :] for h in range(HL)]
    rows = jnp.where(jnp.concatenate(rows * len(CALLS), axis=0) == 1, 1.0, 0.0).astype(bf16)
    slots = XN * NB
    sub = lax.broadcasted_iota(jnp.int32, (slots, BLK), 0)
    lane = lax.broadcasted_iota(jnp.int32, (slots, BLK), 1)
    picked = jnp.zeros((slots, BLK), f32)
    kpos = jnp.full((slots, BLK), -1, jnp.int32)
    for c, js in enumerate(CALLS):
        target = jnp.full((slots, BLK), -1, jnp.int32)
        for r, j in enumerate(js):
            place = (((z - j + ZN) % ZN) * XN + x) * NB + (sub & 3)
            target = jnp.where((sub >> 2) == r, place, target)
        chosen = dot1(jnp.where(lane == target, 1.0, 0.0).astype(bf16), rows, NT)
        picked = jnp.where((lane >> 5) == c, chosen, picked)
        kpos = jnp.where((lane >> 5) == c, target, kpos)
    qpos = z * slots + (lane & 15)
    allowed = (picked > 0.5) & (kpos <= qpos)
    flag = jnp.where(allowed, 1.0, 0.0)
    row16 = lax.broadcasted_iota(jnp.int32, (slots, slots), 0)
    col16 = lax.broadcasted_iota(jnp.int32, (slots, slots), 1)
    earlier = dot1(jnp.where(col16 < row16, 1.0, 0.0).astype(bf16), flag.astype(bf16))
    earlier = jnp.where(allowed, earlier, -1.0)
    value = jnp.where(kpos == qpos, sub + 16, sub).astype(f32)
    total = jnp.sum(flag, axis=0, keepdims=True)
    one = lax.broadcasted_iota(jnp.int32, (1, BLK), 1)
    query = ((one >> 4) & 1) * slots + ((x - ((one >> 2) & 3) + XN) % XN) * NB + (one & 3)
    ranks = 3 * NB // 2

    def nth(p):
        at = jnp.sum(jnp.where(earlier == float(p), value, 0.0), axis=0, keepdims=True)
        return jnp.where(total > float(p), at, 32.0).astype(jnp.int32)

    found = []
    sub8 = lax.broadcasted_iota(jnp.int32, (8, BLK), 0)
    valid = jnp.zeros((8, BLK), f32)
    for p in range(ranks):
        first, second = nth(2 * p), nth(2 * p + 1)
        code = query + ((first & 15) << 6) + ((second & 15) << 10)
        found.append(code + ((first >> 4) << 14) + ((second >> 4) << 16))
        valid = jnp.where((sub8 == p) & (total > float(2 * p)), 1.0, valid)
    ra = lax.broadcasted_iota(jnp.int32, (BLK, BLK), 0)
    ca = lax.broadcasted_iota(jnp.int32, (BLK, BLK), 1)
    same = (ra >> 5) == (ca >> 5)
    valid16 = valid.astype(bf16)
    rank = dot1(valid16, jnp.where(same & (ra < ca), 1.0, 0.0).astype(bf16))
    many = dot1(valid16, jnp.where(same, 1.0, 0.0).astype(bf16))
    used = (many.astype(jnp.int32) + (LANES - 1)) // LANES
    base = jnp.zeros((1, BLK), jnp.int32)
    place = jnp.full((8, BLK), -1.0, f32)
    for p in range(ranks):
        at = base.astype(f32) * float(LANES) + rank
        place = jnp.where((sub8 == p) & (valid > 0.5), at, place)
        base = base + used[p : p + 1]
    ident = jnp.where(ra == ca, 1.0, 0.0).astype(bf16)
    column = dot1(ident, place.astype(bf16), NT)
    spot = lax.broadcasted_iota(jnp.int32, (BLK, SLOTS), 1).astype(f32)
    third = sub // 3
    piece = sub - third * 3
    acc = jnp.zeros((slots, SLOTS), f32)
    for p in range(ranks):
        code = found[p]
        part = jnp.where(piece == 0, code & 255, jnp.where(piece == 1, (code >> 8) & 255, code >> 16))
        part = jnp.where((lane >> 5) == third, part.astype(f32), 0.0)
        part = jnp.where(sub < 12, part, jnp.where((lane >> 5) == sub - 12, 1.0, 0.0))
        hit = jnp.where(column[:, p : p + 1] == spot, 1.0, 0.0).astype(bf16)
        acc = acc + dot1(part.astype(bf16), hit)
    dummy = QB + (2 << 14) + (2 << 16)
    end = lax.broadcasted_iota(jnp.int32, (1, SLOTS), 1)
    for c in range(len(CALLS)):
        low, mid, high = [acc[3 * c + k : 3 * c + k + 1].astype(jnp.int32) for k in range(3)]
        items = low + (mid << 8) + (high << 16)
        items = jnp.where(acc[12 + c : 13 + c] > 0.5, items, dummy)
        count = jnp.max(jnp.where((one >> 5) == c, base, 0), axis=1, keepdims=True)
        out_ref[c : c + 1, :] = jnp.where(end == SLOTS - 1, count, items)


def call(kernel, outs, ins, scratch=(), smem=0, flops=1e9, mib=16):
    size = sum(math.prod(a.shape) * a.dtype.itemsize for a in ins)
    return pl.pallas_call(
        kernel,
        out_shape=outs,
        in_specs=[SMEM] * smem + [VMEM] * (len(ins) - smem),
        out_specs=jax.tree.map(lambda _: VMEM, outs),
        scratch_shapes=list(scratch),
        compiler_params=params(mib),
        cost_estimate=pl.CostEstimate(flops=int(flops), bytes_accessed=size, transcendentals=0),
    )(*ins)


def shape(*dims, dtype=f32):
    return jax.ShapeDtypeStruct(dims, dtype)


def along_z(value, step):
    pairs = [(z * XN + x, ((z + step) % ZN) * XN + x) for z in range(ZN) for x in range(XN)]
    return lax.ppermute(value, "seq", pairs)


def up_z(value, step):
    pairs = [(z * XN + x, (z + step) * XN + x) for z in range(ZN - step) for x in range(XN)]
    return lax.ppermute(value, "seq", pairs)


def along_x(value, step):
    pairs = [(z * XN + x, z * XN + (x + step) % XN) for z in range(ZN) for x in range(XN)]
    return lax.ppermute(value, "seq", pairs)


def sibling(value):
    return lax.ppermute(value, "head", [(g, g ^ 1) for g in range(2 * YN)])


def along_y(value, step):
    pairs = [(g, (g + 2 * step) % (2 * YN)) for g in range(2 * YN)]
    return lax.ppermute(value, "head", pairs)


def ring_z(own):
    rows = [own] + [None] * (ZN - 1)
    for j in range(1, 5):
        rows[j] = along_z(rows[j - 1], 1)
        if j < 4:
            rows[ZN - j] = along_z(rows[(ZN - j + 1) % ZN], -1)
    return rows


def on_device(query, key, value, reflect, block_mask, out_weight):
    here, group = lax.axis_index("seq"), lax.axis_index("head")
    z, x = here // XN, here % XN
    where = jnp.stack([z, x, group // 2, group % 2]).astype(jnp.int32)
    width = out_weight.shape[1] // (2 * YN)
    tokens = query.shape[0]
    tie = lambda *values: lax.optimization_barrier(values)
    square = shape(HL, DH, DH)
    blocks = shape(HL, NB, BLK, DH)
    keys16 = shape(HL, NB, BLK, DH, dtype=bf16)
    v_rows = [value.reshape(NB, BLK, HL, DH).transpose(2, 0, 3, 1)] + [None] * (ZN - 1)
    reflect_h, v_rows[0] = tie(reflect.transpose(1, 0, 2), v_rows[0])
    v_rows[1], v_rows[7] = along_z(v_rows[0], 1), along_z(v_rows[0], -1)
    tri, frames, total = call(
        factor_kernel, (blocks, shape(HL, NB - 1, DH, DH), square), (reflect_h,), flops=2e9
    )
    query, key, block_mask, out_weight, total = tie(query, key, block_mask, out_weight, total)
    others = [along_x(total, k) for k in range(1, XN)]
    q_local, k_local = call(
        local_kernel,
        (blocks, blocks),
        (query.transpose(1, 0, 2), key.transpose(1, 0, 2), reflect_h, tri, frames),
        flops=2e9,
    )
    lists = call(list_kernel, shape(8, SLOTS, dtype=jnp.int32), (where, block_mask), smem=1)
    weight_blocks = out_weight.reshape(-1, 2 * YN, width).transpose(1, 0, 2)
    *others, q_local, k_local, lists, v_rows[1], v_rows[7] = tie(
        *others, q_local, k_local, lists, v_rows[1], v_rows[7]
    )
    before, total = call(
        row_kernel, (shape(XN, HL, DH, DH), square), (where, total, *others), smem=1
    )
    total, q_local, v_rows[1], v_rows[7] = tie(total, q_local, v_rows[1], v_rows[7])
    left = up_z(total, 1)
    q_lanes = [q_local] + [along_x(q_local, k) for k in range(1, XN)]
    v_rows[2], v_rows[6] = along_z(v_rows[1], 1), along_z(v_rows[7], -1)
    left, v_rows[2], v_rows[6] = tie(left, v_rows[2], v_rows[6])
    total, chain = call(partial(hop_kernel, 1), (square, square), (where, left, total), smem=1)
    left = up_z(total, 2)
    v_rows[3], v_rows[5] = along_z(v_rows[2], 1), along_z(v_rows[6], -1)
    left, v_rows[3], v_rows[5] = tie(left, v_rows[3], v_rows[5])
    total, chain = call(
        partial(hop_kernel, 2), (square, square), (where, left, total, chain), smem=1
    )
    left = up_z(total, 4)
    v_rows[4] = along_z(v_rows[5], -1)
    left, weight_blocks, v_rows[4], *q_lanes = tie(left, weight_blocks, v_rows[4], *q_lanes)
    k_turned, chain = call(
        turn_key_kernel, (keys16, square), (where, left, chain, before, k_local), smem=1
    )
    k_rows = ring_z(k_turned)
    queries = call(
        turn_query_kernel, shape(QB + 1, DH, BLK, dtype=bf16), (chain, before, *q_lanes)
    )
    state = (shape(QB + 1, 8, BLK), shape(QB + 1, 8, BLK), shape(QB + 1, DH, BLK))
    carried = ()
    for index, js in enumerate(CALLS):
        last = index == len(CALLS) - 1
        outs = shape(XN, HL * NB, DH + LSE, BLK, dtype=bf16) if last else state
        scratch = [pltpu.VMEM(a.shape, f32) for a in state] if last else []
        scratch += [pltpu.VMEM((len(js), HL, NB, BLK, DH), bf16)] * 2
        scratch += [pltpu.VMEM((3, BLK, BLK), f32), pltpu.VMEM((LANES, 2 * BLK, BLK), bf16)]
        scratch += [pltpu.VMEM((LANES, 8, BLK), f32)]
        carried = call(
            partial(attend_kernel, index, index == 0, last, len(js)),
            outs,
            (lists, queries, *[k_rows[j] for j in js], *[v_rows[j] for j in js], *carried),
            scratch=scratch,
            smem=1,
            flops=2e9 * len(js),
            mib=32,
        )
    got = [carried[0]] + [along_x(carried[a], -a) for a in range(1, XN)]
    sends, mixed = call(
        combine_kernel,
        (shape(YN, tokens, width, dtype=bf16), shape(tokens, HL * DH, dtype=bf16)),
        (where, *got, weight_blocks),
        smem=1,
    )
    other = sibling(sends)
    own = call(own_terms_kernel, shape(YN, tokens, width), (where, mixed, weight_blocks), smem=1)
    part = shape(tokens, width, dtype=bf16)
    keep, *sends = call(
        pair_sum_kernel, (shape(tokens, width), part, part, part), (own, other)
    )
    got = [along_y(sends[k - 1], k) for k in range(1, YN)]
    return call(final_sum_kernel, part, (keep, *got))


def solution(mesh):
    in_specs = (
        P("seq", "head", None),
        P("seq", "head", None),
        P("seq", "head", None),
        P("seq", "head", None),
        P("head", None, None),
        P("head", None),
    )
    out_specs = P("seq", "head")
    return jax.shard_map(
        on_device, mesh=mesh, in_specs=in_specs, out_specs=out_specs, check_vma=False
    )
```

time: 202 us -> 157 us (0.78)
  waiting for transfers between devices: 102 us -> 46.2 us
  between operations: 13.9 us -> 0.41 us
  starting transfers between devices: 28.9 us -> 40.9 us
  Pallas kernels: 48.6 us -> 58.4 us
  local copies, waits for them, and re-layouts: 4.08 us -> 9.4 us
    reduce_scatter x1 -> x0, waiting for transfers between devices: 43.9 us -> none  [on_device(): return lax.psum_scatter(terms, 'head', scatter_dimension=1, tiled=True)]
    ppermute x3, waiting for transfers between devices: 26.8 us -> 9.85 us  [up_z(): return lax.ppermute(value, 'seq', pairs)]
    ppermute x0 -> x4, waiting for transfers between devices: none -> 14.2 us  [the longest x3 12.6 us: along_y(): return lax.ppermute(value, 'head', pairs)]
    ppermute x7 -> x14, waiting for transfers between devices: 18.7 us -> 5.93 us  [along_z(): return lax.ppermute(value, 'seq', pairs)]
    ppermute x7 -> x14, starting transfers between devices: 11.8 us -> 23.8 us  [along_z(): return lax.ppermute(value, 'seq', pairs)]
    pallas_call x8 -> x16, Pallas kernels: 48.6 us -> 58.4 us  [call(): pl.pallas_call(kernel, out_shape=outs, in_specs=[SMEM] * smem + [VMEM] *...]
    ppermute x12 -> x9, waiting for transfers between devices: 12.7 us -> 16.2 us  [along_x(): return lax.ppermute(value, 'seq', pairs)]
    ppermute x0 -> x4, starting transfers between devices: none -> 3.4 us  [the longest x3 3.31 us: along_y(): return lax.ppermute(value, 'head', pairs)]
  transfers between devices with their start and end apart: 24 -> 30, of which waited for: 14 -> 13; matrix products, arithmetic and copies ran while one was open for 2% -> 3% of each run, Pallas kernels for 4% -> 22%
where the time goes in v2:
time: 157 us; the launch traced here: 155 us
  Pallas kernels  58.4 us (37%)
  waiting for transfers between devices  46.2 us (29%)
  starting transfers between devices  40.9 us (26%)
  local copies, waits for them, and re-layouts  9.4 us (6%)
    pallas_call x16, Pallas kernels, call(): pl.pallas_call(kernel, out_shape=outs, in_specs=[SMEM] * smem + [VMEM] *...  58.4 us
    ppermute x14, starting transfers between devices, along_z(): return lax.ppermute(value, 'seq', pairs)  23.8 us
    ppermute x9, waiting for transfers between devices, along_x(): return lax.ppermute(value, 'seq', pairs)  16.2 us
    ppermute x3, waiting for transfers between devices, along_y(): return lax.ppermute(value, 'head', pairs)  12.6 us
    ppermute x9, starting transfers between devices, along_x(): return lax.ppermute(value, 'seq', pairs)  9.86 us
    ppermute x3, waiting for transfers between devices, up_z(): return lax.ppermute(value, 'seq', pairs)  9.85 us
    ppermute x14, waiting for transfers between devices, along_z(): return lax.ppermute(value, 'seq', pairs)  5.93 us
    unnamed x35, local copies, waits for them, and re-layouts  4.34 us
  transfers between devices with their start and end apart: 30, of which 13 were waited for; matrix products, arithmetic and copies ran while one was open for 3% of the time, Pallas kernels for 22%

profile of v2, /device:TPU:224, one launch (start us, length us, event | category | flops | bytes accessed | tf_op | source)
XLA Modules:
  0.0 155.4 jit_solution(4581521866672036986)
XLA Ops:
  2.2 4.2 %shard_map.64 = (f32[2,4,128,128]{3,2,1,0:T(8,128)S(1)}, f32[2,3,128,128]{3,2,1,0:T(8,128)S(1)}, f32[2,128,128]{2,1,0:T(8,128)S(1)}) custom-call(bf16[2,512,128]{2,1,0:T(8,128)(2,1)S(1)} %bitcast.28), custom_call_target="tpu_custom_call" | custom-call | flops 2000000000 | bytes 262144 | tf_op jit(solution)/shard_map/pallas_call | solution.py:393
  8.0 2.7 %collective-permute-start.1 = (f32[2,128,128]{2,1,0:T(8,128)S(1)}, f32[2,128,128]{2,1,0:T(8,128)S(1)}, u32[]{:S(2)}, u32[]{:S(2)}) collective-permute-start(f32[2,128,128]{2,1,0:T(8,128)S(1)} %get-tuple-element.67.own_ref), channel_id=1, source_target_pairs={{0,16},{8,24},{16,0},{24,8},{32,48},{40,56},{48,32},{56,40},{64,80... | collective-permute-start | bytes 393224 | tf_op jit(solution)/shard_map/ppermute | solution.py:420
  12.1 2.0 %collective-permute-start.4 = (bf16[2,4,128,128]{3,2,1,0:T(8,128)(2,1)S(1)}, bf16[2,4,128,128]{3,2,1,0:T(8,128)(2,1)S(1)}, u32[]{:S(2)}, u32[]{:S(2)}) collective-permute-start(bf16[2,4,128,128]{3,2,1,0:T(8,128)(2,1)S(1)} %bitcast.26), channel_id=1, source_target_pairs={{0,224},{8,232},{16,240},{24,248},{32,0},{40,8},{48,16},{56,24},{6... | collective-permute-start | bytes 786440 | tf_op jit(solution)/shard_map/ppermute | solution.py:410
  14.2 3.8 %shard_map.65 = (f32[2,4,128,128]{3,2,1,0:T(8,128)S(1)}, f32[2,4,128,128]{3,2,1,0:T(8,128)S(1)}) custom-call(bf16[2,512,128]{2,1,0:T(8,128)(2,1)S(1)} %get-tuple-element.130.query_ref, bf16[2,512,128]{2,1,0:T(8,128)(2,1)S(1)} %get-tuple-element.129.key_ref, bf16[2,512,128]{2,1,0:T(8,128)(2,1)S(1)} %bitcast.29, ...), custom_call_target="tpu_custom_call" | custom-call | flops 2000000000 | bytes 1703936 | tf_op jit(solution)/shard_map/pallas_call | solution.py:393
  25.2 5.9 %collective-permute-done.5.left_ref = f32[2,128,128]{2,1,0:T(8,128)S(1)} collective-permute-done((f32[2,128,128]{2,1,0:T(8,128)S(1)}, f32[2,128,128]{2,1,0:T(8,128)S(1)}, u32[]{:S(2)}, u32[]{:S(2)}) %collective-permute-start.5) | collective-permute-done | bytes 131104 | tf_op jit(solution)/shard_map/ppermute | solution.py:415
  34.4 3.2 %collective-permute-start.9 = (bf16[2,4,128,128]{3,2,1,0:T(8,128)(2,1)S(1)}, bf16[2,4,128,128]{3,2,1,0:T(8,128)(2,1)S(1)}, u32[]{:S(2)}, u32[]{:S(2)}) collective-permute-start(bf16[2,4,128,128]{3,2,1,0:T(8,128)(2,1)S(1)} %collective-permute-done.6.refs_4_), channel_id=1, source_target_pairs={{0,32},{8,40},{16,48},{24,56},{32,64},{40,72},{48,80},{56,88},{64,... | collective-permute-start | bytes 786440 | tf_op jit(solution)/shard_map/ppermute | solution.py:410
  38.7 4.0 %collective-permute-done.8.left_ref = f32[2,128,128]{2,1,0:T(8,128)S(1)} collective-permute-done((f32[2,128,128]{2,1,0:T(8,128)S(1)}, f32[2,128,128]{2,1,0:T(8,128)S(1)}, u32[]{:S(2)}, u32[]{:S(2)}) %collective-permute-start.8) | collective-permute-done | bytes 131104 | tf_op jit(solution)/shard_map/ppermute | solution.py:415
  44.0 3.7 %collective-permute-start.12 = (bf16[2,4,128,128]{3,2,1,0:T(8,128)(2,1)}, bf16[2,4,128,128]{3,2,1,0:T(8,128)(2,1)}, u32[]{:S(2)}, u32[]{:S(2)}) collective-permute-start(bf16[2,4,128,128]{3,2,1,0:T(8,128)(2,1)} %collective-permute-done.10.refs_6_), channel_id=1, source_target_pairs={{0,224},{8,232},{16,240},{24,248},{32,0},{40,8},{48,16},{56,24},{6... | collective-permute-start | bytes 786440 | tf_op jit(solution)/shard_map/ppermute | solution.py:410
  51.1 2.3 %copy.15 = bf16[256,2048]{0,1:T(8,128)(2,1)} copy(bf16[256,2048]{1,0:T(8,128)(2,1)} %param.11) | data formatting | bytes 2097152 | tf_op jit(solution)/shard_map/optimization_barrier | solution.py:447
  54.9 2.3 %collective-permute-done.13.refs_1_ = f32[2,4,128,128]{3,2,1,0:T(8,128)S(1)} collective-permute-done((f32[2,4,128,128]{3,2,1,0:T(8,128)S(1)}, f32[2,4,128,128]{3,2,1,0:T(8,128)S(1)}, u32[]{:S(2)}, u32[]{:S(2)}) %collective-permute-start.13) | collective-permute-done | bytes 524320 | tf_op jit(solution)/shard_map/ppermute | solution.py:420
  57.2 4.3 %collective-permute-done.15.refs_3_ = f32[2,4,128,128]{3,2,1,0:T(8,128)} collective-permute-done((f32[2,4,128,128]{3,2,1,0:T(8,128)S(1)}, f32[2,4,128,128]{3,2,1,0:T(8,128)}, u32[]{:S(2)}, u32[]{:S(2)}) %collective-permute-start.15) | collective-permute-done | bytes 524320 | tf_op jit(solution)/shard_map/ppermute | solution.py:420
  68.1 4.3 %collective-permute-done.16.refs_2_ = bf16[2,4,128,128]{3,2,1,0:T(8,128)(2,1)S(1)} collective-permute-done((bf16[2,4,128,128]{3,2,1,0:T(8,128)(2,1)S(1)}, bf16[2,4,128,128]{3,2,1,0:T(8,128)(2,1)S(1)}, u32[]{:S(2)}, u32[]{:S(2)}) %collective-permute-start.16) | collective-permute-done | bytes 262176 | tf_op jit(solution)/shard_map/ppermute | solution.py:410
  72.3 2.8 %collective-permute-start.17 = (bf16[2,4,128,128]{3,2,1,0:T(8,128)(2,1)S(1)}, bf16[2,4,128,128]{3,2,1,0:T(8,128)(2,1)S(1)}, u32[]{:S(2)}, u32[]{:S(2)}) collective-permute-start(bf16[2,4,128,128]{3,2,1,0:T(8,128)(2,1)S(1)} %collective-permute-done.16.refs_2_), channel_id=1, source_target_pairs={{0,32},{8,40},{16,48},{24,56},{32,64},{40,72},{48,80},{56,88},{64,... | collective-permute-start | bytes 786440 | tf_op jit(solution)/shard_map/ppermute | solution.py:410
  75.2 3.4 %shard_map.71.refs_1_ = bf16[33,128,128]{2,1,0:T(8,128)(2,1)S(1)} custom-call(f32[2,128,128]{2,1,0:T(8,128)S(1)} %get-tuple-element.101.chain_ref, f32[4,2,128,128]{3,2,1,0:T(8,128)S(1)} %get-tuple-element.99.before_ref, f32[2,4,128,128]{3,2,1,0:T(8,128)S(1)} %get-tuple-element.102.refs_0_, f32[2,4,128,128]{3,2,1,0:T(8,128)S(1)} %collective-permute-done.13.refs_1_, ...), custom_call_target="tpu_custom_call" | custom-call | flops 1000000000 | bytes 2752512 | tf_op jit(solution)/shard_map/pallas_call | solution.py:393
  78.6 5.1 %shard_map.72 = (f32[33,8,128]{2,1,0:T(8,128)S(1)}, f32[33,8,128]{2,1,0:T(8,128)S(1)}, f32[33,128,128]{2,1,0:T(8,128)S(1)}) custom-call(s32[8,256]{1,0:T(8,128)S(1)} %shard_map.66.refs_0_, bf16[33,128,128]{2,1,0:T(8,128)(2,1)S(1)} %shard_map.71.refs_1_, bf16[2,4,128,128]{3,2,1,0:T(8,128)(2,1)S(1)} %get-tuple-element.106.refs_2_, ...), custom_call_target="tpu_custom_call" | custom-call | flops 2000000000 | bytes 1613824 | tf_op jit(solution)/shard_map/pallas_call | solution.py:393
  84.2 2.8 %collective-permute-start.18 = (bf16[2,4,128,128]{3,2,1,0:T(8,128)(2,1)S(1)}, bf16[2,4,128,128]{3,2,1,0:T(8,128)(2,1)S(1)}, u32[]{:S(2)}, u32[]{:S(2)}) collective-permute-start(bf16[2,4,128,128]{3,2,1,0:T(8,128)(2,1)S(1)} %collective-permute-done.17.refs_2_), channel_id=1, source_target_pairs={{0,32},{8,40},{16,48},{24,56},{32,64},{40,72},{48,80},{56,88},{64,... | collective-permute-start | bytes 786440 | tf_op jit(solution)/shard_map/ppermute | solution.py:410
  87.0 9.1 %shard_map.73 = (f32[33,8,128]{2,1,0:T(8,128)S(1)}, f32[33,8,128]{2,1,0:T(8,128)S(1)}, f32[33,128,128]{2,1,0:T(8,128)S(1)}) custom-call(s32[8,256]{1,0:T(8,128)S(1)} %shard_map.66.refs_0_, bf16[33,128,128]{2,1,0:T(8,128)(2,1)S(1)} %shard_map.71.refs_1_, bf16[2,4,128,128]{3,2,1,0:T(8,128)(2,1)S(1)} %collective-permute-done.16.refs_2_, ...), custom_call_target="tpu_custom_call" | custom-call | flops 4000000000 | bytes 4571136 | tf_op jit(solution)/shard_map/pallas_call | solution.py:393
  96.2 3.2 %collective-permute-start.22 = (bf16[2,4,128,128]{3,2,1,0:T(8,128)(2,1)S(1)}, bf16[2,4,128,128]{3,2,1,0:T(8,128)(2,1)S(1)}, u32[]{:S(2)}, u32[]{:S(2)}) collective-permute-start(bf16[2,4,128,128]{3,2,1,0:T(8,128)(2,1)S(1)} %collective-permute-done.18.refs_2_), channel_id=1, source_target_pairs={{0,32},{8,40},{16,48},{24,56},{32,64},{40,72},{48,80},{56,88},{64,... | collective-permute-start | bytes 786440 | tf_op jit(solution)/shard_map/ppermute | solution.py:410
  99.5 9.0 %shard_map.74 = (f32[33,8,128]{2,1,0:T(8,128)S(1)}, f32[33,8,128]{2,1,0:T(8,128)S(1)}, f32[33,128,128]{2,1,0:T(8,128)S(1)}) custom-call(s32[8,256]{1,0:T(8,128)S(1)} %shard_map.66.refs_0_, bf16[33,128,128]{2,1,0:T(8,128)(2,1)S(1)} %shard_map.71.refs_1_, bf16[2,4,128,128]{3,2,1,0:T(8,128)(2,1)S(1)} %collective-permute-done.17.refs_2_, ...), custom_call_target="tpu_custom_call" | custom-call | flops 4000000000 | bytes 4571136 | tf_op jit(solution)/shard_map/pallas_call | solution.py:393
  108.5 14.0 %shard_map.75 = bf16[4,8,144,128]{3,2,1,0:T(8,128)(2,1)S(1)} custom-call(s32[8,256]{1,0:T(8,128)S(1)} %shard_map.66.refs_0_, bf16[33,128,128]{2,1,0:T(8,128)(2,1)S(1)} %shard_map.71.refs_1_, bf16[2,4,128,128]{3,2,1,0:T(8,128)(2,1)S(1)} %collective-permute-done.18.refs_2_, bf16[2,4,128,128]{3,2,1,0:T(8,128)(2,1)S(1)} %collective-permute-done.21.refs_3_, ...), custom_call_target="tpu_custom_call" | custom-call | flops 6000000000 | bytes 5095424 | tf_op jit(solution)/shard_map/pallas_call | solution.py:393
  124.9 4.5 %collective-permute-done.23.refs_1_ = bf16[8,144,128]{2,1,0:T(8,128)(2,1)S(1)} collective-permute-done((bf16[8,144,128]{2,1,0:T(8,128)(2,1)S(1)}, bf16[8,144,128]{2,1,0:T(8,128)(2,1)S(1)}, u32[]{:S(2)}, u32[]{:S(2)}) %collective-permute-start.23) | collective-permute-done | bytes 294944 | tf_op jit(solution)/shard_map/ppermute | solution.py:420
  129.4 2.1 %collective-permute-done.24.refs_2_ = bf16[8,144,128]{2,1,0:T(8,128)(2,1)S(1)} collective-permute-done((bf16[8,144,128]{2,1,0:T(8,128)(2,1)S(1)}, bf16[8,144,128]{2,1,0:T(8,128)(2,1)S(1)}, u32[]{:S(2)}, u32[]{:S(2)}) %collective-permute-start.24) | collective-permute-done | bytes 294944 | tf_op jit(solution)/shard_map/ppermute | solution.py:420
  131.5 3.1 %collective-permute-done.25.refs_3_ = bf16[8,144,128]{2,1,0:T(8,128)(2,1)S(1)} collective-permute-done((bf16[8,144,128]{2,1,0:T(8,128)(2,1)S(1)}, bf16[8,144,128]{2,1,0:T(8,128)(2,1)S(1)}, u32[]{:S(2)}, u32[]{:S(2)}) %collective-permute-start.25) | collective-permute-done | bytes 294944 | tf_op jit(solution)/shard_map/ppermute | solution.py:420
  142.0 11.9 %collective-permute-done.27.one_ref = bf16[512,256]{1,0:T(8,128)(2,1)S(1)} collective-permute-done((bf16[512,256]{1,0:T(8,128)(2,1)S(1)}, bf16[512,256]{1,0:T(8,128)(2,1)S(1)}, u32[]{:S(2)}, u32[]{:S(2)}) %collective-permute-start.27) | collective-permute-done | bytes 262176 | tf_op jit(solution)/shard_map/ppermute | solution.py:429
  (93 shorter events, 41.4 us)
Async XLA Ops:
  6.4 13.1 %collective-permute-start = (f32[2,128,128]{2,1,0:T(8,128)S(1)}, f32[2,128,128]{2,1,0:T(8,128)S(1)}, u32[]{:S(2)}, u32[]{:S(2)}) collective-permute-start(f32[2,128,128]{2,1,0:T(8,128)S(1)} %get-tuple-element.67.own_ref), channel_id=1, source_target_pairs={{0,8},{8,16},{16,24},{24,0},{32,40},{40,48},{48,56},{56,32},{64,72... | collective-permute-start | bytes 393224 | tf_op jit(solution)/shard_map/ppermute | solution.py:420
  8.0 11.6 %collective-permute-start.1 = (f32[2,128,128]{2,1,0:T(8,128)S(1)}, f32[2,128,128]{2,1,0:T(8,128)S(1)}, u32[]{:S(2)}, u32[]{:S(2)}) collective-permute-start(f32[2,128,128]{2,1,0:T(8,128)S(1)} %get-tuple-element.67.own_ref), channel_id=1, source_target_pairs={{0,16},{8,24},{16,0},{24,8},{32,48},{40,56},{48,32},{56,40},{64,80... | collective-permute-start | bytes 393224 | tf_op jit(solution)/shard_map/ppermute | solution.py:420
  10.7 8.8 %collective-permute-start.2 = (f32[2,128,128]{2,1,0:T(8,128)S(1)}, f32[2,128,128]{2,1,0:T(8,128)S(1)}, u32[]{:S(2)}, u32[]{:S(2)}) collective-permute-start(f32[2,128,128]{2,1,0:T(8,128)S(1)} %get-tuple-element.67.own_ref), channel_id=1, source_target_pairs={{0,24},{8,0},{16,8},{24,16},{32,56},{40,32},{48,40},{56,48},{64,88... | collective-permute-start | bytes 393224 | tf_op jit(solution)/shard_map/ppermute | solution.py:420
  12.1 8.4 %collective-permute-start.4 = (bf16[2,4,128,128]{3,2,1,0:T(8,128)(2,1)S(1)}, bf16[2,4,128,128]{3,2,1,0:T(8,128)(2,1)S(1)}, u32[]{:S(2)}, u32[]{:S(2)}) collective-permute-start(bf16[2,4,128,128]{3,2,1,0:T(8,128)(2,1)S(1)} %bitcast.26), channel_id=1, source_target_pairs={{0,224},{8,232},{16,240},{24,248},{32,0},{40,8},{48,16},{56,24},{6... | collective-permute-start | bytes 786440 | tf_op jit(solution)/shard_map/ppermute | solution.py:410
  21.8 9.3 %collective-permute-start.6 = (bf16[2,4,128,128]{3,2,1,0:T(8,128)(2,1)S(1)}, bf16[2,4,128,128]{3,2,1,0:T(8,128)(2,1)S(1)}, u32[]{:S(2)}, u32[]{:S(2)}) collective-permute-start(bf16[2,4,128,128]{3,2,1,0:T(8,128)(2,1)S(1)} %collective-permute-done.3.refs_4_), channel_id=1, source_target_pairs={{0,32},{8,40},{16,48},{24,56},{32,64},{40,72},{48,80},{56,88},{64,... | collective-permute-start | bytes 786440 | tf_op jit(solution)/shard_map/ppermute | solution.py:410
  22.2 8.9 %collective-permute-start.7 = (bf16[2,4,128,128]{3,2,1,0:T(8,128)(2,1)S(1)}, bf16[2,4,128,128]{3,2,1,0:T(8,128)(2,1)S(1)}, u32[]{:S(2)}, u32[]{:S(2)}) collective-permute-start(bf16[2,4,128,128]{3,2,1,0:T(8,128)(2,1)S(1)} %collective-permute-done.4.refs_5_), channel_id=1, source_target_pairs={{0,224},{8,232},{16,240},{24,248},{32,0},{40,8},{48,16},{56,24},{6... | collective-permute-start | bytes 786440 | tf_op jit(solution)/shard_map/ppermute | solution.py:410
  31.9 10.8 %collective-permute-start.8 = (f32[2,128,128]{2,1,0:T(8,128)S(1)}, f32[2,128,128]{2,1,0:T(8,128)S(1)}, u32[]{:S(2)}, u32[]{:S(2)}) collective-permute-start(f32[2,128,128]{2,1,0:T(8,128)S(1)} %get-tuple-element.88.total_ref), channel_id=1, source_target_pairs={{0,64},{8,72},{16,80},{24,88},{32,96},{40,104},{48,112},{56,120},{... | collective-permute-start | bytes 393224 | tf_op jit(solution)/shard_map/ppermute | solution.py:415
  33.2 24.0 %collective-permute-start.13 = (f32[2,4,128,128]{3,2,1,0:T(8,128)S(1)}, f32[2,4,128,128]{3,2,1,0:T(8,128)S(1)}, u32[]{:S(2)}, u32[]{:S(2)}) collective-permute-start(f32[2,4,128,128]{3,2,1,0:T(8,128)S(1)} %get-tuple-element.102.refs_0_), channel_id=1, source_target_pairs={{0,8},{8,16},{16,24},{24,0},{32,40},{40,48},{48,56},{56,32},{64,72... | collective-permute-start | bytes 1572872 | tf_op jit(solution)/shard_map/ppermute | solution.py:420
  33.8 8.9 %collective-permute-start.10 = (bf16[2,4,128,128]{3,2,1,0:T(8,128)(2,1)S(1)}, bf16[2,4,128,128]{3,2,1,0:T(8,128)(2,1)}, u32[]{:S(2)}, u32[]{:S(2)}) collective-permute-start(bf16[2,4,128,128]{3,2,1,0:T(8,128)(2,1)S(1)} %collective-permute-done.7.refs_5_), channel_id=1, source_target_pairs={{0,224},{8,232},{16,240},{24,248},{32,0},{40,8},{48,16},{56,24},{6... | collective-permute-start | bytes 786440 | tf_op jit(solution)/shard_map/ppermute | solution.py:410
  34.4 9.0 %collective-permute-start.9 = (bf16[2,4,128,128]{3,2,1,0:T(8,128)(2,1)S(1)}, bf16[2,4,128,128]{3,2,1,0:T(8,128)(2,1)S(1)}, u32[]{:S(2)}, u32[]{:S(2)}) collective-permute-start(bf16[2,4,128,128]{3,2,1,0:T(8,128)(2,1)S(1)} %collective-permute-done.6.refs_4_), channel_id=1, source_target_pairs={{0,32},{8,40},{16,48},{24,56},{32,64},{40,72},{48,80},{56,88},{64,... | collective-permute-start | bytes 786440 | tf_op jit(solution)/shard_map/ppermute | solution.py:410
  37.5 19.6 %collective-permute-start.14 = (f32[2,4,128,128]{3,2,1,0:T(8,128)S(1)}, f32[2,4,128,128]{3,2,1,0:T(8,128)S(1)}, u32[]{:S(2)}, u32[]{:S(2)}) collective-permute-start(f32[2,4,128,128]{3,2,1,0:T(8,128)S(1)} %get-tuple-element.102.refs_0_), channel_id=1, source_target_pairs={{0,16},{8,24},{16,0},{24,8},{32,48},{40,56},{48,32},{56,40},{64,80... | collective-permute-start | bytes 1572872 | tf_op jit(solution)/shard_map/ppermute | solution.py:420
  42.7 18.8 %collective-permute-start.15 = (f32[2,4,128,128]{3,2,1,0:T(8,128)S(1)}, f32[2,4,128,128]{3,2,1,0:T(8,128)}, u32[]{:S(2)}, u32[]{:S(2)}) collective-permute-start(f32[2,4,128,128]{3,2,1,0:T(8,128)S(1)} %get-tuple-element.102.refs_0_), channel_id=1, source_target_pairs={{0,24},{8,0},{16,8},{24,16},{32,56},{40,32},{48,40},{56,48},{64,88... | collective-permute-start | bytes 1572872 | tf_op jit(solution)/shard_map/ppermute | solution.py:420
  44.0 17.4 %collective-permute-start.12 = (bf16[2,4,128,128]{3,2,1,0:T(8,128)(2,1)}, bf16[2,4,128,128]{3,2,1,0:T(8,128)(2,1)}, u32[]{:S(2)}, u32[]{:S(2)}) collective-permute-start(bf16[2,4,128,128]{3,2,1,0:T(8,128)(2,1)} %collective-permute-done.10.refs_6_), channel_id=1, source_target_pairs={{0,224},{8,232},{16,240},{24,248},{32,0},{40,8},{48,16},{56,24},{6... | collective-permute-start | bytes 786440 | tf_op jit(solution)/shard_map/ppermute | solution.py:410
  49.9 11.6 %collective-permute-start.11 = (f32[2,128,128]{2,1,0:T(8,128)}, f32[2,128,128]{2,1,0:T(8,128)S(1)}, u32[]{:S(2)}, u32[]{:S(2)}) collective-permute-start(f32[2,128,128]{2,1,0:T(8,128)} %get-tuple-element.93), channel_id=1, source_target_pairs={{0,128},{8,136},{16,144},{24,152},{32,160},{40,168},{48,176},{56,1... | collective-permute-start | bytes 393224 | tf_op jit(solution)/shard_map/ppermute | solution.py:415
  67.1 16.6 %collective-permute-start.19 = (bf16[2,4,128,128]{3,2,1,0:T(8,128)(2,1)S(1)}, bf16[2,4,128,128]{3,2,1,0:T(8,128)(2,1)S(1)}, u32[]{:S(2)}, u32[]{:S(2)}) collective-permute-start(bf16[2,4,128,128]{3,2,1,0:T(8,128)(2,1)S(1)} %get-tuple-element.106.refs_2_), channel_id=1, source_target_pairs={{0,224},{8,232},{16,240},{24,248},{32,0},{40,8},{48,16},{56,24},{6... | collective-permute-start | bytes 786440 | tf_op jit(solution)/shard_map/ppermute | solution.py:410
  72.3 11.9 %collective-permute-start.17 = (bf16[2,4,128,128]{3,2,1,0:T(8,128)(2,1)S(1)}, bf16[2,4,128,128]{3,2,1,0:T(8,128)(2,1)S(1)}, u32[]{:S(2)}, u32[]{:S(2)}) collective-permute-start(bf16[2,4,128,128]{3,2,1,0:T(8,128)(2,1)S(1)} %collective-permute-done.16.refs_2_), channel_id=1, source_target_pairs={{0,32},{8,40},{16,48},{24,56},{32,64},{40,72},{48,80},{56,88},{64,... | collective-permute-start | bytes 786440 | tf_op jit(solution)/shard_map/ppermute | solution.py:410
  83.7 12.4 %collective-permute-start.20 = (bf16[2,4,128,128]{3,2,1,0:T(8,128)(2,1)S(1)}, bf16[2,4,128,128]{3,2,1,0:T(8,128)(2,1)S(1)}, u32[]{:S(2)}, u32[]{:S(2)}) collective-permute-start(bf16[2,4,128,128]{3,2,1,0:T(8,128)(2,1)S(1)} %collective-permute-done.19.refs_3_), channel_id=1, source_target_pairs={{0,224},{8,232},{16,240},{24,248},{32,0},{40,8},{48,16},{56,24},{6... | collective-permute-start | bytes 786440 | tf_op jit(solution)/shard_map/ppermute | solution.py:410
  84.2 12.0 %collective-permute-start.18 = (bf16[2,4,128,128]{3,2,1,0:T(8,128)(2,1)S(1)}, bf16[2,4,128,128]{3,2,1,0:T(8,128)(2,1)S(1)}, u32[]{:S(2)}, u32[]{:S(2)}) collective-permute-start(bf16[2,4,128,128]{3,2,1,0:T(8,128)(2,1)S(1)} %collective-permute-done.17.refs_2_), channel_id=1, source_target_pairs={{0,32},{8,40},{16,48},{24,56},{32,64},{40,72},{48,80},{56,88},{64,... | collective-permute-start | bytes 786440 | tf_op jit(solution)/shard_map/ppermute | solution.py:410
  96.1 12.4 %collective-permute-start.21 = (bf16[2,4,128,128]{3,2,1,0:T(8,128)(2,1)S(1)}, bf16[2,4,128,128]{3,2,1,0:T(8,128)(2,1)S(1)}, u32[]{:S(2)}, u32[]{:S(2)}) collective-permute-start(bf16[2,4,128,128]{3,2,1,0:T(8,128)(2,1)S(1)} %collective-permute-done.20.refs_3_), channel_id=1, source_target_pairs={{0,224},{8,232},{16,240},{24,248},{32,0},{40,8},{48,16},{56,24},{6... | collective-permute-start | bytes 786440 | tf_op jit(solution)/shard_map/ppermute | solution.py:410
  96.2 12.3 %collective-permute-start.22 = (bf16[2,4,128,128]{3,2,1,0:T(8,128)(2,1)S(1)}, bf16[2,4,128,128]{3,2,1,0:T(8,128)(2,1)S(1)}, u32[]{:S(2)}, u32[]{:S(2)}) collective-permute-start(bf16[2,4,128,128]{3,2,1,0:T(8,128)(2,1)S(1)} %collective-permute-done.18.refs_2_), channel_id=1, source_target_pairs={{0,32},{8,40},{16,48},{24,56},{32,64},{40,72},{48,80},{56,88},{64,... | collective-permute-start | bytes 786440 | tf_op jit(solution)/shard_map/ppermute | solution.py:410
  124.9 9.7 %collective-permute-start.25 = (bf16[8,144,128]{2,1,0:T(8,128)(2,1)S(1)}, bf16[8,144,128]{2,1,0:T(8,128)(2,1)S(1)}, u32[]{:S(2)}, u32[]{:S(2)}) collective-permute-start(bf16[8,144,128]{2,1,0:T(8,128)(2,1)S(1)} %get-tuple-element.125), channel_id=1, source_target_pairs={{0,8},{8,16},{16,24},{24,0},{32,40},{40,48},{48,56},{56,32},{64,72... | collective-permute-start | bytes 884744 | tf_op jit(solution)/shard_map/ppermute | solution.py:420
  138.7 15.3 %collective-permute-start.27 = (bf16[512,256]{1,0:T(8,128)(2,1)S(1)}, bf16[512,256]{1,0:T(8,128)(2,1)S(1)}, u32[]{:S(2)}, u32[]{:S(2)}) collective-permute-start(bf16[512,256]{1,0:T(8,128)(2,1)S(1)} %get-tuple-element.122), channel_id=1, source_target_pairs={{0,2},{1,3},{2,4},{3,5},{4,6},{5,7},{6,0},{7,1},{8,10},{9,11},{10,... | collective-permute-start | bytes 786440 | tf_op jit(solution)/shard_map/ppermute | solution.py:429
  138.8 15.2 %collective-permute-start.28 = (bf16[512,256]{1,0:T(8,128)(2,1)S(1)}, bf16[512,256]{1,0:T(8,128)(2,1)S(1)}, u32[]{:S(2)}, u32[]{:S(2)}) collective-permute-start(bf16[512,256]{1,0:T(8,128)(2,1)S(1)} %get-tuple-element.123), channel_id=1, source_target_pairs={{0,4},{1,5},{2,6},{3,7},{4,0},{5,1},{6,2},{7,3},{8,12},{9,13},{10,... | collective-permute-start | bytes 786440 | tf_op jit(solution)/shard_map/ppermute | solution.py:429
  140.3 14.3 %collective-permute-start.29 = (bf16[512,256]{1,0:T(8,128)(2,1)S(1)}, bf16[512,256]{1,0:T(8,128)(2,1)S(1)}, u32[]{:S(2)}, u32[]{:S(2)}) collective-permute-start(bf16[512,256]{1,0:T(8,128)(2,1)S(1)} %get-tuple-element.124), channel_id=1, source_target_pairs={{0,6},{1,7},{2,0},{3,1},{4,2},{5,3},{6,4},{7,5},{8,14},{9,15},{10,... | collective-permute-start | bytes 786440 | tf_op jit(solution)/shard_map/ppermute | solution.py:429
  (23 other events, 174.6 us)
